TPU v7x, 512 devices: a whole 4x8x8 slice. The times are simulated.
512 devices in a mesh: lon: 32 (over z_hi, x, core), lat: 16 (over y, z_lo).
Axes of the slice: x: 4, y: 8, z: 8 (z_hi: 4, z_lo: 2; z = z_hi * 2 + z_lo), core: 2. Of those that a mesh axis runs over, the one named last changes fastest.
Arguments:
- field: bfloat16 [256, 256, 4096], P(None, 'lat', 'lon'), may hold values from -6 to 6
- cotangent: bfloat16 [256, 256, 4096], P(None, 'lat', 'lon'), may hold values from -6 to 6
- filters: bfloat16 [3, 256, 3, 17], P(None, 'lat'), may hold values from -1.5 to 1.5
- reach: int32 [256, 2], P('lat'), may hold values from -8 to 8, as said below
- mixing: bfloat16 [256, 3, 256], replicated, may hold values from -0.21875 to 0.21875
- bias: float32 [256], replicated, may hold values from -3 to 3
Outputs:
- out_field: bfloat16 [256, 256, 4096], P(None, 'lat', 'lon')
- grad_field: bfloat16 [256, 256, 4096], P(None, 'lat', 'lon')
- grad_mixing: float32 [256, 3, 256], P('lon')
Inputs may be any that keep to these rules, and one draw needn't show every extreme that they name: Row i's filter support in longitude runs from offset reach[i, 0] to reach[i, 1]; it always holds offsets -1, 0 and 1, and the first and last rows of the grid span -8 to 8.
All inputs are finite; a program needn't handle non-finite values.
Results may differ from a plain program's by a relative error of at most 0.0056.
Values may be sent and summed in bfloat16 or wider, within the bound.
No kernel may reach another device: no remote copies, remote signals or barrier semaphores. Data moves between devices by JAX's collectives and lax.ppermute only.
A program may use at most 64 MiB of HBM per device.

v0:
```python
import math

import jax
import jax.numpy as jnp
from jax import lax
from jax.sharding import PartitionSpec as P

K = 3
SMAX = 8


def extended(cells, sides, width, closed):
    for axis, dim in sides:
        count = lax.axis_size(axis)
        ends = count if closed else count - 1
        head = lax.slice_in_dim(cells, 0, width, axis=dim)
        tail = lax.slice_in_dim(cells, cells.shape[dim] - width, cells.shape[dim], axis=dim)
        cells = jnp.concatenate(
            [
                lax.ppermute(tail, axis, [(i, (i + 1) % count) for i in range(ends)]),
                cells,
                lax.ppermute(head, axis, [((i + 1) % count, i) for i in range(ends)]),
            ],
            axis=dim,
        )
    return cells


def gelu_pair(pre):
    root = 0.7978845608028654
    inner = root * (pre + 0.044715 * pre * pre * pre)
    tanh_v = jnp.tanh(inner)
    value = 0.5 * pre * (1.0 + tanh_v)
    slope = 0.5 * (1.0 + tanh_v) + 0.5 * pre * (1.0 - tanh_v * tanh_v) * root * (
        1.0 + 3.0 * 0.044715 * pre * pre
    )
    return (value, slope)


def body(field, cotangent, filters, reach, mixing, bias):
    chans, rows, cols = field.shape
    taps = 2 * SMAX + 1
    wide = cols + 2 * SMAX
    total_rows = rows * lax.axis_size("lat")
    total_cols = cols * lax.axis_size("lon")
    offsets = jnp.arange(taps, dtype=jnp.int32) - SMAX
    inside = (reach[:, 0:1] <= offsets[None, :]) & (offsets[None, :] <= reach[:, 1:2])
    coef = filters * inside[None, :, None, :].astype(jnp.bfloat16)
    pos_p = jnp.arange(wide, dtype=jnp.int32)[None, :, None]
    pos_q = jnp.arange(cols, dtype=jnp.int32)[None, None, :]
    tap_ids = jnp.arange(taps, dtype=jnp.int32)[:, None, None]
    shift_table = (pos_p - pos_q == tap_ids).astype(jnp.bfloat16)
    band = jnp.einsum(
        "kldt,tpq->ldkpq", coef, shift_table, preferred_element_type=jnp.float32
    ).astype(jnp.bfloat16)
    beside_all = extended(field, (("lon", 2),), SMAX, True)
    padded = extended(beside_all, (("lat", 1),), 1, False)
    acc = jnp.zeros((K, chans, rows, cols), jnp.float32)
    for offset_row in range(3):
        acc = acc + jnp.einsum(
            "clp,lkpq->kclq",
            padded[:, offset_row : offset_row + rows],
            band[:, offset_row],
            preferred_element_type=jnp.float32,
        )
    basis = acc.astype(jnp.bfloat16)
    pre = (
        jnp.einsum("okc,kclq->olq", mixing, basis, preferred_element_type=jnp.float32)
        + bias[:, None, None]
    )
    value, slope = gelu_pair(pre)
    out_field = (field.astype(jnp.float32) + value).astype(jnp.bfloat16)
    cot32 = cotangent.astype(jnp.float32)
    grad_pre = (cot32 * slope).astype(jnp.bfloat16)
    scale = 1.0 / math.sqrt(total_rows * total_cols)
    share = chans // lax.axis_size("lon")
    summed = lax.psum(
        jnp.einsum("olq,kclq->okc", grad_pre, basis, preferred_element_type=jnp.float32) * scale,
        ("lon", "lat"),
    )
    grad_mixing = lax.dynamic_slice_in_dim(summed, lax.axis_index("lon") * share, share, 0)
    back = jnp.einsum("okc,olq->kclq", mixing, grad_pre, preferred_element_type=jnp.float32).astype(
        jnp.bfloat16
    )
    back_wide = extended(back, (("lon", 3),), SMAX, True)
    back_pad = extended(back_wide, (("lat", 2),), 1, False)
    coef_pad = extended(coef, (("lat", 1),), 1, False)
    mirror_table = (pos_p - pos_q == 2 * SMAX - tap_ids).astype(jnp.bfloat16)
    inner = jnp.zeros((chans, rows, cols), jnp.float32)
    for offset_row in range(3):
        low = 2 - offset_row
        mirror_band = jnp.einsum(
            "klt,tpq->lkpq",
            coef_pad[:, low : low + rows, offset_row],
            mirror_table,
            preferred_element_type=jnp.float32,
        ).astype(jnp.bfloat16)
        inner = inner + jnp.einsum(
            "kclp,lkpq->clq",
            back_pad[:, :, low : low + rows],
            mirror_band,
            preferred_element_type=jnp.float32,
        )
    grad_field = (cot32 + inner).astype(jnp.bfloat16)
    return (out_field, grad_field, grad_mixing)


def solution(mesh):
    placed = (
        P(None, "lat", "lon"),
        P(None, "lat", "lon"),
        P(None, "lat", None, None),
        P("lat", None),
        P(),
        P(),
    )
    return jax.shard_map(
        body,
        mesh=mesh,
        in_specs=placed,
        out_specs=(P(None, "lat", "lon"), P(None, "lat", "lon"), P("lon", None, None)),
        check_vma=False,
    )
```

profile of v0, /device:TPU:1, one launch (start us, length us, event | category | flops | bytes accessed | tf_op | source)
XLA Modules:
  0.0 361.9 jit_solution(15997497335458490001)
XLA Ops:
  7.2 0.0 copy-start
  7.2 0.0 copy-start.8
  7.2 0.0 copy-start.7
  7.2 0.0 all-reduce.2.cloned.1.call-start
  7.2 1.7 copy.9
  8.9 0.6 fusion.83
  9.6 4.5 %collective-permute-start = (bf16[256,16,8]{0,2,1:T(8,128)(2,1)}, bf16[256,16,8]{0,2,1:T(8,128)(2,1)S(1)}, u32[]{:S(2)}, u32[]{:S(2)}) collective-permute-start(bf16[256,16,8]{0,2,1:T(8,128)(2,1)} %get-tuple-element.15), channel_id=1, source_target_pairs={{0,16},{16,32},{32,48},{48,64},{64,80},{80,96},{96,112},{112,128},... | collective-permute-start | bytes 196616 | tf_op jit(solution)/shard_map/ppermute | solution.py:20
  14.1 6.2 %collective-permute-start.1 = (bf16[256,16,8]{0,2,1:T(8,128)(2,1)S(1)}, bf16[256,16,8]{0,2,1:T(8,128)(2,1)S(1)}, u32[]{:S(2)}, u32[]{:S(2)}) collective-permute-start(bf16[256,16,8]{0,2,1:T(8,128)(2,1)S(1)} %get-tuple-element.16), channel_id=1, source_target_pairs={{16,0},{32,16},{48,32},{64,48},{80,64},{96,80},{112,96},{128,112},... | collective-permute-start | bytes 196616 | tf_op jit(solution)/shard_map/ppermute | solution.py:22
  20.3 0.0 copy-done.8
  20.3 0.1 and_convert_fusion
  20.4 0.0 copy-done.7
  20.4 1.3 collective-permute-start.4
  21.7 4.0 %collective-permute-start.8 = (bf16[3,1,3,17]{3,1,2,0:T(2,128)(2,1)S(1)}, bf16[3,1,3,17]{3,1,2,0:T(2,128)(2,1)S(1)}, u32[]{:S(2)}, u32[]{:S(2)}) collective-permute-start(bf16[3,1,3,17]{3,1,2,0:T(2,128)(2,1)S(1)} %get-tuple-element.17), channel_id=1, source_target_pairs={{0,1},{1,2},{2,3},{3,4},{4,5},{5,6},{6,7},{7,8},{8,9},{9,10},{10,1... | collective-permute-start | bytes 926 | tf_op jit(solution)/shard_map/ppermute | solution.py:20
  25.7 1.5 convert_bitcast_fusion
  27.3 2.8 slice_bitcast_fusion
  30.0 2.4 copy.16
  32.4 1.9 fusion.36
  34.4 0.0 collective-permute-done.4
  34.4 1.9 fusion.38
  36.3 0.0 copy-start.2
  36.3 0.0 collective-permute-done.8
  36.3 1.9 fusion.34
  38.2 0.0 collective-permute-done
  38.2 0.0 collective-permute-done.1
  38.2 0.1 pad_maximum_fusion.24
  38.3 1.9 collective-permute-start.2
  40.2 1.5 collective-permute-start.3
  41.7 0.0 copy-done.2
  41.7 0.0 copy-start.1
  41.7 1.2 fusion.28
  43.0 0.0 collective-permute-done.2
  43.0 0.2 copy-done.1
  43.2 1.2 fusion.30
  44.4 0.9 collective-permute-done.3
  45.3 2.2 fusion.10
  47.5 0.0 copy-done
  47.5 0.0 copy-done.9
  47.5 0.0 copy-start.5
  47.5 2.4 add_convert_fusion.1
  49.9 0.0 copy-done.5
  49.9 2.2 convert_bitcast_fusion.1
  52.2 0.8 fusion.81
  53.0 4.3 %collective-permute-start.5 = (bf16[3,256,16,8]{1,3,0,2:T(8,128)(2,1)}, bf16[3,256,16,8]{1,3,0,2:T(8,128)(2,1)}, u32[]{:S(2)}, u32[]{:S(2)}) collective-permute-start(bf16[3,256,16,8]{1,3,0,2:T(8,128)(2,1)} %get-tuple-element.11), channel_id=1, source_target_pairs={{0,16},{16,32},{32,48},{48,64},{64,80},{80,96},{96,112},{112,128},... | collective-permute-start | bytes 589832 | tf_op jit(solution)/shard_map/ppermute | solution.py:20
  57.3 8.9 %collective-permute-start.6 = (bf16[3,256,16,8]{1,3,0,2:T(8,128)(2,1)}, bf16[3,256,16,8]{1,3,0,2:T(8,128)(2,1)}, u32[]{:S(2)}, u32[]{:S(2)}) collective-permute-start(bf16[3,256,16,8]{1,3,0,2:T(8,128)(2,1)} %get-tuple-element.12), channel_id=1, source_target_pairs={{16,0},{32,16},{48,32},{64,48},{80,64},{96,80},{112,96},{128,112},... | collective-permute-start | bytes 589832 | tf_op jit(solution)/shard_map/ppermute | solution.py:22
  66.2 2.7 fusion.43
  68.9 0.0 all-reduce.2.cloned.1.call-update
  68.9 2.6 copy.19
  71.6 0.0 collective-permute-done.5
  71.6 0.0 collective-permute-done.6
  71.6 1.7 pad_maximum_fusion.25
  73.3 1.3 collective-permute-start.7
  74.5 4.7 %collective-permute-start.9 = (bf16[3,256,1,144]{1,3,0,2:T(8,128)(2,1)}, bf16[3,256,1,144]{1,3,0,2:T(8,128)(2,1)}, u32[]{:S(2)}, u32[]{:S(2)}) collective-permute-start(bf16[3,256,1,144]{1,3,0,2:T(8,128)(2,1)} %get-tuple-element.9), channel_id=1, source_target_pairs={{0,1},{1,2},{2,3},{3,4},{4,5},{5,6},{6,7},{7,8},{8,9},{9,10},{10,1... | collective-permute-start | bytes 663560 | tf_op jit(solution)/shard_map/ppermute | solution.py:20
  79.2 0.0 copy-done.4
  79.2 3.4 fusion.4
  82.6 261.6 %all-reduce.2.cloned.1.call-done = f32[256,3,256]{2,0,1:T(8,128)} async-done(((f32[256,3,256]{2,0,1:T(8,128)}), f32[256,3,256]{2,0,1:T(8,128)}) %all-reduce.2.cloned.1.call-update) | async-done | bytes 786448 | tf_op jit(solution)/shard_map/psum | solution.py:77
  344.3 1.3 constant_dynamic-slice_fusion
  345.6 0.0 collective-permute-done.7
  345.6 2.8 fusion.2
  348.5 0.0 collective-permute-done.9
  348.5 0.0 copy-done.3
  348.5 0.0 copy-done.6
  348.5 0.3 copy-done.10
  348.8 3.6 fusion.12
  352.4 2.6 copy.20
  (12 shorter events, 0.1 us)
Async XLA Ops:
  7.2 40.3 %copy-start = (bf16[256,3,256]{2,0,1:T(8,128)(2,1)S(1)}, bf16[256,3,256]{2,0,1:T(8,128)(2,1)}, u32[]{:S(2)}) copy-start(bf16[256,3,256]{2,0,1:T(8,128)(2,1)} %param.10) | copy-start | bytes 1179652
  7.2 13.1 %copy-start.8 = (s32[16,2]{0,1:T(2,128)S(1)}, s32[16,2]{0,1:T(2,128)}, u32[]{:S(2)}) copy-start(s32[16,2]{0,1:T(2,128)} %param.9) | copy-start | bytes 388
  7.2 13.2 %copy-start.7 = (bf16[3,16,3,17]{3,1,2,0:T(8,128)(2,1)S(1)}, bf16[3,16,3,17]{3,1,2,0:T(8,128)(2,1)}, u32[]{:S(2)}) copy-start(bf16[3,16,3,17]{3,1,2,0:T(8,128)(2,1)} %param.8) | copy-start | bytes 14692
  7.2 337.1 %all-reduce.2.cloned.1.call-start = ((), (), s32[]{:S(2)}) async-start(), calls=%async_computation | async-start | bytes 1572864 | tf_op jit(solution)/shard_map/psum | solution.py:77
  9.6 28.6 %collective-permute-start = (bf16[256,16,8]{0,2,1:T(8,128)(2,1)}, bf16[256,16,8]{0,2,1:T(8,128)(2,1)S(1)}, u32[]{:S(2)}, u32[]{:S(2)}) collective-permute-start(bf16[256,16,8]{0,2,1:T(8,128)(2,1)} %get-tuple-element.15), channel_id=1, source_target_pairs={{0,16},{16,32},{32,48},{48,64},{64,80},{80,96},{96,112},{112,128},... | collective-permute-start | bytes 196616 | tf_op jit(solution)/shard_map/ppermute | solution.py:20
  14.1 24.1 %collective-permute-start.1 = (bf16[256,16,8]{0,2,1:T(8,128)(2,1)S(1)}, bf16[256,16,8]{0,2,1:T(8,128)(2,1)S(1)}, u32[]{:S(2)}, u32[]{:S(2)}) collective-permute-start(bf16[256,16,8]{0,2,1:T(8,128)(2,1)S(1)} %get-tuple-element.16), channel_id=1, source_target_pairs={{16,0},{32,16},{48,32},{64,48},{80,64},{96,80},{112,96},{128,112},... | collective-permute-start | bytes 196616 | tf_op jit(solution)/shard_map/ppermute | solution.py:22
  20.4 13.9 %collective-permute-start.4 = (bf16[3,1,3,17]{3,1,2,0:T(2,128)(2,1)S(1)}, bf16[3,1,3,17]{3,1,2,0:T(2,128)(2,1)S(1)}, u32[]{:S(2)}, u32[]{:S(2)}) collective-permute-start(bf16[3,1,3,17]{3,1,2,0:T(2,128)(2,1)S(1)} %get-tuple-element.18), channel_id=1, source_target_pairs={{1,0},{2,1},{3,2},{4,3},{5,4},{6,5},{7,6},{8,7},{9,8},{10,9},{11,1... | collective-permute-start | bytes 926 | tf_op jit(solution)/shard_map/ppermute | solution.py:22
  21.7 14.6 %collective-permute-start.8 = (bf16[3,1,3,17]{3,1,2,0:T(2,128)(2,1)S(1)}, bf16[3,1,3,17]{3,1,2,0:T(2,128)(2,1)S(1)}, u32[]{:S(2)}, u32[]{:S(2)}) collective-permute-start(bf16[3,1,3,17]{3,1,2,0:T(2,128)(2,1)S(1)} %get-tuple-element.17), channel_id=1, source_target_pairs={{0,1},{1,2},{2,3},{3,4},{4,5},{5,6},{6,7},{7,8},{8,9},{9,10},{10,1... | collective-permute-start | bytes 926 | tf_op jit(solution)/shard_map/ppermute | solution.py:20
  36.3 5.4 %copy-start.2 = (bf16[16,3,144,128]{3,0,1,2:T(8,128)(2,1)S(1)}, bf16[16,3,144,128]{3,0,1,2:T(8,128)(2,1)}, u32[]{:S(2)}) copy-start(bf16[16,3,144,128]{3,0,1,2:T(8,128)(2,1)} %get-tuple-element.7) | copy-start | bytes 5308420
  38.3 4.7 %collective-permute-start.2 = (bf16[256,1,144]{0,2,1:T(8,128)(2,1)S(1)}, bf16[256,1,144]{0,2,1:T(8,128)(2,1)S(1)}, u32[]{:S(2)}, u32[]{:S(2)}) collective-permute-start(bf16[256,1,144]{0,2,1:T(8,128)(2,1)S(1)} %get-tuple-element.14), channel_id=1, source_target_pairs={{0,1},{1,2},{2,3},{3,4},{4,5},{5,6},{6,7},{7,8},{8,9},{9,10},{10,1... | collective-permute-start | bytes 221192 | tf_op jit(solution)/shard_map/ppermute | solution.py:20
  40.2 5.1 %collective-permute-start.3 = (bf16[256,1,144]{0,2,1:T(8,128)(2,1)S(1)}, bf16[256,1,144]{0,2,1:T(8,128)(2,1)S(1)}, u32[]{:S(2)}, u32[]{:S(2)}) collective-permute-start(bf16[256,1,144]{0,2,1:T(8,128)(2,1)S(1)} %get-tuple-element.13), channel_id=1, source_target_pairs={{1,0},{2,1},{3,2},{4,3},{5,4},{6,5},{7,6},{8,7},{9,8},{10,9},{11,1... | collective-permute-start | bytes 221192 | tf_op jit(solution)/shard_map/ppermute | solution.py:22
  41.7 1.5 copy-start.1
  45.3 2.2 copy-start.9
  47.5 2.4 copy-start.5
  53.0 18.6 %collective-permute-start.5 = (bf16[3,256,16,8]{1,3,0,2:T(8,128)(2,1)}, bf16[3,256,16,8]{1,3,0,2:T(8,128)(2,1)}, u32[]{:S(2)}, u32[]{:S(2)}) collective-permute-start(bf16[3,256,16,8]{1,3,0,2:T(8,128)(2,1)} %get-tuple-element.11), channel_id=1, source_target_pairs={{0,16},{16,32},{32,48},{48,64},{64,80},{80,96},{96,112},{112,128},... | collective-permute-start | bytes 589832 | tf_op jit(solution)/shard_map/ppermute | solution.py:20
  57.3 14.3 %collective-permute-start.6 = (bf16[3,256,16,8]{1,3,0,2:T(8,128)(2,1)}, bf16[3,256,16,8]{1,3,0,2:T(8,128)(2,1)}, u32[]{:S(2)}, u32[]{:S(2)}) collective-permute-start(bf16[3,256,16,8]{1,3,0,2:T(8,128)(2,1)} %get-tuple-element.12), channel_id=1, source_target_pairs={{16,0},{32,16},{48,32},{64,48},{80,64},{96,80},{112,96},{128,112},... | collective-permute-start | bytes 589832 | tf_op jit(solution)/shard_map/ppermute | solution.py:22
  71.6 7.7 %copy-start.4 = (bf16[144,128,3,16]{1,3,2,0:T(8,128)(2,1)S(1)}, bf16[144,128,3,16]{1,3,2,0:T(8,128)(2,1)}, u32[]{:S(2)}) copy-start(bf16[144,128,3,16]{1,3,2,0:T(8,128)(2,1)} %fusion.36) | copy-start | bytes 5308420
  73.3 272.4 %collective-permute-start.7 = (bf16[3,256,1,144]{1,3,0,2:T(8,128)(2,1)}, bf16[3,256,1,144]{1,3,0,2:T(8,128)(2,1)}, u32[]{:S(2)}, u32[]{:S(2)}) collective-permute-start(bf16[3,256,1,144]{1,3,0,2:T(8,128)(2,1)} %get-tuple-element.10), channel_id=1, source_target_pairs={{1,0},{2,1},{3,2},{4,3},{5,4},{6,5},{7,6},{8,7},{9,8},{10,9},{11,1... | collective-permute-start | bytes 663560 | tf_op jit(solution)/shard_map/ppermute | solution.py:22
  74.5 273.9 %collective-permute-start.9 = (bf16[3,256,1,144]{1,3,0,2:T(8,128)(2,1)}, bf16[3,256,1,144]{1,3,0,2:T(8,128)(2,1)}, u32[]{:S(2)}, u32[]{:S(2)}) collective-permute-start(bf16[3,256,1,144]{1,3,0,2:T(8,128)(2,1)} %get-tuple-element.9), channel_id=1, source_target_pairs={{0,1},{1,2},{2,3},{3,4},{4,5},{5,6},{6,7},{7,8},{8,9},{9,10},{10,1... | collective-permute-start | bytes 663560 | tf_op jit(solution)/shard_map/ppermute | solution.py:20
  345.6 2.9 copy-start.3
  345.6 2.9 copy-start.6
  345.6 3.2 copy-start.10
Sparse Core Ops, SparseCore 0:
  69.0 275.1 all-reduce.1
where the time goes:
time: 363 us; the launch traced here: 362 us
  waiting for transfers between devices  263 us (72%)
  starting transfers between devices  38.6 us (11%)
  matrix products  29 us (8%)
  local copies, waits for them, and re-layouts  15.5 us (4%)
  between operations  14.3 us (4%)
    psum x1, waiting for transfers between devices, body(): lax.psum(jnp.einsum('olq,kclq->okc', grad_pre, basis, preferred_element_t...  262 us
    ppermute x5, starting transfers between devices, extended(): lax.ppermute(tail, axis, [(i, (i + 1) % count) for i in range(ends)])  19.4 us
    ppermute x5, starting transfers between devices, extended(): lax.ppermute(head, axis, [((i + 1) % count, i) for i in range(ends)])  19.1 us
    unnamed x26, local copies, waits for them, and re-layouts  9.94 us
    dot_general x3, matrix products, body(): jnp.einsum('kclp,lkpq->clq', back_pad[:, :, low:low + rows], mirror_band,...  9.82 us
  transfers between devices with their start and end apart: 11, of which 2 were waited for; matrix products, arithmetic and copies ran while one was open for 8% of the time, Pallas kernels for 0%

commit v1 on v0

v1 whole, which is shorter than its diff:
```python
import math

import jax
import jax.numpy as jnp
from jax import lax
from jax.sharding import PartitionSpec as P

K = 3
SMAX = 8
TAPS = 2 * SMAX + 1


def swap_edges(first, last, axis, closed):
    count = lax.axis_size(axis)
    odd = lax.axis_index(axis) % 2 == 1
    near = [(j, j ^ 1) for j in range(count)]
    far = []
    for j in range(1, count, 2):
        if closed or j + 1 < count:
            far += [(j, (j + 1) % count), ((j + 1) % count, j)]
    got_near = lax.ppermute(jnp.where(odd, first, last), axis, near)
    got_far = lax.ppermute(jnp.where(odd, last, first), axis, far)
    return jnp.where(odd, got_near, got_far), jnp.where(odd, got_far, got_near)


def gelu_pair(pre):
    root = 0.7978845608028654
    inner = root * (pre + 0.044715 * pre * pre * pre)
    tanh_v = jnp.tanh(inner)
    value = 0.5 * pre * (1.0 + tanh_v)
    slope = 0.5 * (1.0 + tanh_v) + 0.5 * pre * (1.0 - tanh_v * tanh_v) * root * (
        1.0 + 3.0 * 0.044715 * pre * pre
    )
    return (value, slope)


def coef_message(row):
    flat = row.reshape(1, K * 3 * TAPS)
    return jnp.pad(flat, ((0, 15), (0, 256 - K * 3 * TAPS)))


def body(field, cotangent, filters, reach, mixing, bias):
    chans, rows, cols = field.shape
    total_rows = rows * lax.axis_size("lat")
    total_cols = cols * lax.axis_size("lon")
    offsets = jnp.arange(TAPS, dtype=jnp.int32) - SMAX
    inside = (reach[:, 0:1] <= offsets[None, :]) & (offsets[None, :] <= reach[:, 1:2])
    coef = filters * inside[None, :, None, :].astype(jnp.bfloat16)
    field_t = jnp.transpose(field, (1, 2, 0))
    cot_t = jnp.transpose(cotangent, (1, 2, 0))
    two, one = 2 * SMAX, SMAX
    left, right = swap_edges(
        jnp.concatenate([field_t[:, :two], cot_t[:, :one]], axis=1),
        jnp.concatenate([field_t[:, cols - two :], cot_t[:, cols - one :]], axis=1),
        "lon",
        True,
    )
    wide_f = cols + 2 * two
    wide_c = cols + 2 * one
    fx = jnp.concatenate([left[:, :two], field_t, right[:, :two]], axis=1)
    cx = jnp.concatenate([left[:, two:], cot_t, right[:, two:]], axis=1)
    above, below = swap_edges(
        jnp.concatenate(
            [fx[:2].reshape(2 * wide_f, chans), cx[0], coef_message(coef[:, 0])], axis=0
        ),
        jnp.concatenate(
            [
                fx[rows - 2 :].reshape(2 * wide_f, chans),
                cx[rows - 1],
                coef_message(coef[:, rows - 1]),
            ],
            axis=0,
        ),
        "lat",
        False,
    )

    def parts(block):
        f = block[: 2 * wide_f].reshape(2, wide_f, chans)
        c = block[2 * wide_f : 2 * wide_f + wide_c][None]
        k = block[2 * wide_f + wide_c, : K * 3 * TAPS].reshape(K, 1, 3, TAPS)
        return f, c, k

    f_up, c_up, k_up = parts(above)
    f_dn, c_dn, k_dn = parts(below)
    fx = jnp.concatenate([f_up, fx, f_dn], axis=0)
    cx = jnp.concatenate([c_up, cx, c_dn], axis=0)
    coef = jnp.concatenate([k_up, coef, k_dn], axis=1)

    pos_p = jnp.arange(wide_f, dtype=jnp.int32)[None, :, None]
    pos_q = jnp.arange(wide_c, dtype=jnp.int32)[None, None, :]
    pos_b = jnp.arange(cols, dtype=jnp.int32)[None, None, :]
    tap_ids = jnp.arange(TAPS, dtype=jnp.int32)[:, None, None]
    table = (pos_p - pos_q == tap_ids).astype(jnp.bfloat16)
    mirror = (pos_q.reshape(1, wide_c, 1) - pos_b == 2 * SMAX - tap_ids).astype(jnp.bfloat16)
    tall = rows + 2
    band = jnp.einsum("kldt,tpq->ldkpq", coef, table, preferred_element_type=jnp.float32).astype(
        jnp.bfloat16
    )
    acc = 0.0
    for r in range(3):
        acc = acc + jnp.einsum(
            "lpc,lkpq->klqc", fx[r : r + tall], band[:, r], preferred_element_type=jnp.float32
        )
    basis = acc.astype(jnp.bfloat16)
    pre = (
        jnp.einsum("okc,klqc->lqo", mixing, basis, preferred_element_type=jnp.float32)
        + bias[None, None, :]
    )
    value, slope = gelu_pair(pre)
    grad_pre = (cx.astype(jnp.float32) * slope).astype(jnp.bfloat16)
    out_t = (field_t.astype(jnp.float32) + value[1:-1, one : one + cols]).astype(jnp.bfloat16)

    scale = 1.0 / math.sqrt(total_rows * total_cols)
    n_lon, n_lat = lax.axis_size("lon"), lax.axis_size("lat")
    share = chans // n_lon
    term = (
        jnp.einsum(
            "lqo,klqc->okc",
            grad_pre[1:-1, one : one + cols],
            basis[:, 1:-1, one : one + cols],
            preferred_element_type=jnp.float32,
        )
        * scale
    ).astype(jnp.bfloat16)
    got = lax.all_to_all(term.reshape(n_lon, share, K * chans), "lon", 0, 0)
    part = jnp.sum(got.astype(jnp.float32), axis=0).astype(jnp.bfloat16)
    got = lax.all_to_all(jnp.broadcast_to(part[None], (n_lat, share, K * chans)), "lat", 0, 0)
    grad_mixing = jnp.sum(got.astype(jnp.float32), axis=0).reshape(share, K, chans)

    spread = 0.0
    for r in range(3):
        low = 2 - r
        mband = jnp.einsum(
            "klt,tqb->lkqb", coef[:, low : low + rows, r], mirror, preferred_element_type=jnp.float32
        ).astype(jnp.bfloat16)
        spread = spread + jnp.einsum(
            "lqo,lkqb->klbo",
            grad_pre[low : low + rows],
            mband,
            preferred_element_type=jnp.float32,
        )
    inner = jnp.einsum(
        "okc,klbo->lbc", mixing, spread.astype(jnp.bfloat16), preferred_element_type=jnp.float32
    )
    grad_t = (cot_t.astype(jnp.float32) + inner).astype(jnp.bfloat16)
    return (jnp.transpose(out_t, (2, 0, 1)), jnp.transpose(grad_t, (2, 0, 1)), grad_mixing)


def solution(mesh):
    placed = (
        P(None, "lat", "lon"),
        P(None, "lat", "lon"),
        P(None, "lat", None, None),
        P("lat", None),
        P(),
        P(),
    )
    return jax.shard_map(
        body,
        mesh=mesh,
        in_specs=placed,
        out_specs=(P(None, "lat", "lon"), P(None, "lat", "lon"), P("lon", None, None)),
        check_vma=False,
    )
```

time: 363 us -> 128 us (0.35)
  waiting for transfers between devices: 263 us -> 11.4 us
  matrix products: 29 us -> 51.9 us
  between operations: 14.3 us -> 0.99 us
  other arithmetic: 1.87 us -> 7.83 us
    psum x1 -> x0, waiting for transfers between devices: 262 us -> none  [body(): lax.psum(jnp.einsum('olq,kclq->okc', grad_pre, basis, preferred_element_t...]
    all_to_all x0 -> x2, starting transfers between devices: none -> 25.6 us  [the longest x1 15.8 us: body(): got = lax.all_to_all(term.reshape(n_lon, share, K * chans), 'lon', 0, 0)]
    ppermute x10 -> x4, starting transfers between devices: 38.5 us -> 13.3 us  [the longest x2 10.7 us: swap_edges(): got_near = lax.ppermute(jnp.where(odd, first, last), axis, near)]
    dot_general x13 -> x12, matrix products: 29 us -> 51.9 us  [the longest x3 15.2 us: body(): jnp.einsum('lpc,lkpq->klqc', fx[r:r + tall], band[:, r], preferred_elemen...]
    ppermute x10 -> x4, waiting for transfers between devices: 0.94 us -> 6.41 us  [the longest x2 3.99 us: swap_edges(): got_far = lax.ppermute(jnp.where(odd, last, first), axis, far)]
    all_to_all x0 -> x2, waiting for transfers between devices: none -> 5.04 us  [the longest x1 5.03 us: body(): lax.all_to_all(jnp.broadcast_to(part[None], (n_lat, share, K * chans)), '...]
    unnamed x26 -> x28, local copies, waits for them, and re-layouts: 9.94 us -> 6.45 us
  transfers between devices with their start and end apart: 11 -> 6, of which waited for: 2 -> 3; matrix products, arithmetic and copies ran while one was open for 8% -> 22% of each run, Pallas kernels for 0% -> 0%
where the time goes in v1:
time: 128 us; the launch traced here: 127 us
  matrix products  51.9 us (41%)
  starting transfers between devices  38.9 us (30%)
  local copies, waits for them, and re-layouts  15.6 us (12%)
  waiting for transfers between devices  11.4 us (9%)
  other arithmetic  7.83 us (6%)
    all_to_all x1, starting transfers between devices, body(): got = lax.all_to_all(term.reshape(n_lon, share, K * chans), 'lon', 0, 0)  15.8 us
    dot_general x3, matrix products, body(): jnp.einsum('lpc,lkpq->klqc', fx[r:r + tall], band[:, r], preferred_elemen...  15.2 us
    ppermute x2, starting transfers between devices, swap_edges(): got_near = lax.ppermute(jnp.where(odd, first, last), axis, near)  10.7 us
    dot_general x2, matrix products, body(): jnp.einsum('lqo,lkqb->klbo', grad_pre[low:low + rows], mband, preferred_e...  10.6 us
    all_to_all x1, starting transfers between devices, body(): lax.all_to_all(jnp.broadcast_to(part[None], (n_lat, share, K * chans)), '...  9.79 us
    dot_general x1, matrix products, body(): jnp.einsum('okc,klbo->lbc', mixing, spread.astype(jnp.bfloat16), preferre...  7.68 us
    dot_general x1, matrix products, body(): jnp.einsum('okc,klqc->lqo', mixing, basis, preferred_element_type=jnp.flo...  7.29 us
    unnamed x28, local copies, waits for them, and re-layouts  6.45 us
  transfers between devices with their start and end apart: 6, of which 3 were waited for; matrix products, arithmetic and copies ran while one was open for 22% of the time, Pallas kernels for 0%

profile of v1, /device:TPU:1, one launch (start us, length us, event | category | flops | bytes accessed | tf_op | source)
XLA Modules:
  0.0 126.7 jit_solution(18406580764824482413)
XLA Ops:
  0.6 0.0 copy-start
  0.6 0.0 copy-start.7
  0.7 0.0 copy-start.10
  0.7 1.7 %copy.34 = bf16[256,16,128]{0,2,1:T(8,128)(2,1)S(1)} copy(bf16[256,16,128]{2,1,0:T(8,128)(2,1)} %param.6) | data formatting | bytes 2097152 | tf_op args[0]
  2.4 0.7 fusion.111
  3.1 0.0 copy-done.7
  3.1 0.8 copy.35
  3.9 0.0 copy-start.1
  4.0 1.4 %broadcast_select_fusion.7 = (bf16[16,24,256]{2,1,0:T(8,128)(2,1)S(1)}, bf16[16,24,256]{2,1,0:T(8,128)(2,1)S(1)}) fusion(pred[]{:T(512)S(6)} %eq.51, bf16[16,8,256]{2,1,0:T(8,128)(2,1)S(1)} %get-tuple-element.27, bf16[16,16,256]{2,1,0:T(8,128)(2,1)} %get-tuple-element.25, bf16[16,8,256]{2,1,0:T(8,128)(2,1)S(1)} %get-tuple-element.26, ...), kind=kLoop, calls=%fused_computation.107 | loop fusion | flops 983040 | bytes 786433 | tf_op jit(solution)/shard_map/jit(_where)/select_n | solution.py:21
  5.4 8.8 %collective-permute-start = (bf16[16,24,256]{2,1,0:T(8,128)(2,1)S(1)}, bf16[16,24,256]{2,1,0:T(8,128)(2,1)S(1)}, u32[]{:S(2)}, u32[]{:S(2)}) collective-permute-start(bf16[16,24,256]{2,1,0:T(8,128)(2,1)S(1)} %get-tuple-element.34), channel_id=1, source_target_pairs={{0,16},{16,0},{32,48},{48,32},{64,80},{80,64},{96,112},{112,96},{1... | collective-permute-start | bytes 589832 | tf_op jit(solution)/shard_map/ppermute | solution.py:21
  14.2 1.9 %collective-permute-start.1 = (bf16[16,24,256]{2,1,0:T(8,128)(2,1)S(1)}, bf16[16,24,256]{2,1,0:T(8,128)(2,1)}, u32[]{:S(2)}, u32[]{:S(2)}) collective-permute-start(bf16[16,24,256]{2,1,0:T(8,128)(2,1)S(1)} %get-tuple-element.35), channel_id=1, source_target_pairs={{16,32},{32,16},{48,64},{64,48},{80,96},{96,80},{112,128},{128,112... | collective-permute-start | bytes 589832 | tf_op jit(solution)/shard_map/ppermute | solution.py:22
  16.1 0.0 copy-done.10
  16.2 0.1 and_convert_fusion
  16.2 0.8 broadcast_multiply_fusion
  17.1 0.1 reshape_squeeze.12
  17.1 0.1 reshape_squeeze.13
  17.3 0.0 collective-permute-done
  17.3 4.0 %collective-permute-done.1 = bf16[16,24,256]{2,1,0:T(8,128)(2,1)} collective-permute-done((bf16[16,24,256]{2,1,0:T(8,128)(2,1)S(1)}, bf16[16,24,256]{2,1,0:T(8,128)(2,1)}, u32[]{:S(2)}, u32[]{:S(2)}) %collective-permute-start.1) | collective-permute-done | bytes 196640 | tf_op jit(solution)/shard_map/ppermute | solution.py:22
  21.3 1.0 broadcast_select_fusion.5
  22.3 0.0 copy-start.9
  22.4 0.0 copy-done.1
  22.4 0.1 broadcast_select_fusion.3
  22.5 1.9 %collective-permute-start.2 = (bf16[480,256]{1,0:T(8,128)(2,1)S(1)}, bf16[480,256]{1,0:T(8,128)(2,1)S(1)}, u32[]{:S(2)}, u32[]{:S(2)}) collective-permute-start(bf16[480,256]{1,0:T(8,128)(2,1)S(1)} %get-tuple-element.30), channel_id=1, source_target_pairs={{0,1},{1,0},{2,3},{3,2},{4,5},{5,4},{6,7},{7,6},{8,9},{9,8},{10,11... | collective-permute-start | bytes 737288 | tf_op jit(solution)/shard_map/ppermute | solution.py:21
  24.4 0.7 collective-permute-start.3
  25.1 1.9 %convert_bitcast_fusion.2 = bf16[16,3,144,128]{3,0,1,2:T(8,128)(2,1)} fusion(s32[144,128]{1,0:T(8,128)S(1)} %iota_subtract_fusion.1, s32[17]{0:T(128)S(1)} %iota_subtract_fusion.2, bf16[3,16,3,17]{3,1,2,0:T(8,128)(2,1)S(1)} %broadcast_multiply_fusion), kind=kOutput, calls=%fused_computation.43 | convolution fusion | flops 31279104 | bytes 1856000 | tf_op jit(solution)/shard_map/klt,tqb->lkqb/dot_general | solution.py:134
  27.0 0.0 copy-done.9
  27.0 2.4 %collective-permute-done.2 = bf16[480,256]{1,0:T(8,128)(2,1)S(1)} collective-permute-done((bf16[480,256]{1,0:T(8,128)(2,1)S(1)}, bf16[480,256]{1,0:T(8,128)(2,1)S(1)}, u32[]{:S(2)}, u32[]{:S(2)}) %collective-permute-start.2) | collective-permute-done | bytes 245792 | tf_op jit(solution)/shard_map/ppermute | solution.py:21
  29.4 0.0 collective-permute-done.3
  29.5 0.7 slice.161
  30.2 0.7 slice_bitcast_fusion.12
  30.8 0.1 reshape_squeeze.16
  30.9 0.1 reshape_squeeze.17
  31.0 1.9 %convert_bitcast_fusion.3 = bf16[16,3,144,128]{3,0,1,2:T(8,128)(2,1)} fusion(s32[144,128]{1,0:T(8,128)S(1)} %iota_subtract_fusion.1, s32[17]{0:T(128)S(1)} %iota_subtract_fusion.2, bf16[3,1,3,17]{3,1,2,0:T(2,128)(2,1)S(1)} %reshape_squeeze.17, bf16[3,16,3,17]{3,1,2,0:T(8,128)(2,1)S(1)} %broadcast_multiply_fusion), kind=kOutput, calls=%fused_computation.44 | convolution fusion | flops 31282368 | bytes 1848470 | tf_op jit(solution)/shard_map/klt,tqb->lkqb/dot_general | solution.py:134
  32.9 1.9 %convert_bitcast_fusion.1 = bf16[16,3,144,128]{3,0,1,2:T(8,128)(2,1)} fusion(s32[144,128]{1,0:T(8,128)S(1)} %iota_subtract_fusion.1, s32[17]{0:T(128)S(1)} %iota_subtract_fusion.2, bf16[3,16,3,17]{3,1,2,0:T(8,128)(2,1)S(1)} %broadcast_multiply_fusion, bf16[3,1,3,17]{3,1,2,0:T(2,128)(2,1)S(1)} %reshape_squeeze.16), kind=kOutput, calls=%fused_computation.42 | convolution fusion | flops 31282368 | bytes 1848470 | tf_op jit(solution)/shard_map/klt,tqb->lkqb/dot_general | solution.py:134
  34.8 4.4 %convert_bitcast_fusion = bf16[18,3,3,160,144]{3,0,1,2,4:T(8,128)(2,1)S(1)} fusion(s32[160,144]{0,1:T(8,128)S(1)} %iota_subtract_fusion, bf16[3,1,3,17]{3,1,2,0:T(2,128)(2,1)S(1)} %reshape_squeeze.17, bf16[3,16,3,17]{3,1,2,0:T(8,128)(2,1)S(1)} %broadcast_multiply_fusion, bf16[3,1,3,17]{3,1,2,0:T(2,128)(2,1)S(1)} %reshape_squeeze.16), kind=kOutput, calls=%fused_computation | convolution fusion | flops 131045008 | bytes 7562628 | tf_op jit(solution)/shard_map/kldt,tpq->ldkpq/dot_general | solution.py:97
  39.3 4.4 %slice_bitcast_fusion.2 = (bf16[18,3,160,144]{2,0,1,3:T(8,128)(2,1)}, bf16[18,3,160,144]{2,0,1,3:T(8,128)(2,1)S(1)}, bf16[18,3,160,144]{2,0,1,3:T(8,128)(2,1)}) fusion(bf16[18,3,3,160,144]{3,0,1,2,4:T(8,128)(2,1)S(1)} %convert_bitcast_fusion), kind=kLoop, calls=%fused_computation.5 | loop fusion | bytes 14929920 | tf_op jit(solution)/shard_map/squeeze | solution.py:103
  43.7 2.3 %fusion.1 = f32[18,3,144,256]{3,2,1,0:T(8,128)S(1)} fusion(bf16[18,3,160,144]{2,0,1,3:T(8,128)(2,1)S(1)} %get-tuple-element.15, bf16[2,160,256]{2,1,0:T(8,128)(2,1)} %bitcast.167, bf16[16,16,256]{2,1,0:T(8,128)(2,1)S(1)} %slice.151, bf16[16,128,256]{2,1,0:T(8,128)(2,1)S(1)} %bitcast.157, bf16[16,16,256]{2,1,0:T(8,128)(2,1)S(1)} %slice.150), kind=kOutput, calls=%fused_computation.7 | convolution fusion | flops 642908160 | bytes 11925504 | tf_op jit(solution)/shard_map/lpc,lkpq->klqc/dot_general | solution.py:102
  45.9 0.3 copy-done.5
  46.2 0.0 copy-done.8
  46.2 4.3 %fusion.3 = f32[18,3,144,256]{3,2,1,0:T(8,128)} fusion(bf16[18,3,160,144]{2,0,1,3:T(8,128)(2,1)S(1)} %copy-done.5, bf16[2,160,256]{2,1,0:T(8,128)(2,1)S(1)} %bitcast.168, bf16[2,160,256]{2,1,0:T(8,128)(2,1)S(1)} %bitcast.163, bf16[16,16,256]{2,1,0:T(8,128)(2,1)S(1)} %slice.151, bf16[16,128,256]{2,1,0:T(8,128)(2,1)S(1)} %bitcast.158, ...), kind=kOutput, calls=%fused_computation.9 | convolution fusion | flops 644382720 | bytes 12089344 | tf_op jit(solution)/shard_map/lpc,lkpq->klqc/dot_general | solution.py:102
  50.5 8.6 %fusion = bf16[3,18,144,256]{3,2,0,1:T(8,128)(2,1)} fusion(f32[18,3,144,256]{3,2,1,0:T(8,128)S(1)} %fusion.1, f32[18,3,144,256]{3,2,1,0:T(8,128)} %fusion.3, bf16[18,3,160,144]{2,0,1,3:T(8,128)(2,1)} %get-tuple-element.14, bf16[16,16,256]{2,1,0:T(8,128)(2,1)S(1)} %slice.151, bf16[16,128,256]{2,1,0:T(8,128)(2,1)S(1)} %bitcast.159, ...), kind=kOutput, calls=%fused_computation.6 | convolution fusion | flops 648880128 | bytes 23869440 | tf_op jit(solution)/shard_map/lpc,lkpq->klqc/dot_general | solution.py:102
  59.2 0.0 copy-done
  59.2 0.0 copy-done.11
  59.2 7.3 %fusion.22 = (bf16[18,144,256]{2,1,0:T(8,128)(2,1)S(1)}, f32[18,144,256]{2,1,0:T(8,128)}, f32[18,144,256]{2,1,0:T(8,128)}) fusion(bf16[1,144,256]{2,1,0:T(8,128)(2,1)} %get-tuple-element.38, bf16[16,8,256]{2,1,0:T(8,128)(2,1)} %copy-done.9, bf16[16,128,256]{2,1,0:T(8,128)(2,1)} %bitcast.162, bf16[16,8,256]{2,1,0:T(8,128)(2,1)S(1)} %slice.152, ...), kind=kOutput, calls=%fused_computation.27 | convolution fusion | flops 1039122432 | bytes 12338176 | tf_op jit(solution)/shard_map/okc,klqc->lqo/dot_general | solution.py:107
  66.5 0.0 copy-done.6
  66.5 1.0 fusion.77
  67.5 0.3 copy.49
  67.9 1.2 reshape.126
  69.1 15.8 %all-to-all-start = ((bf16[32,8,768]{2,1,0:T(8,128)(2,1)}), bf16[32,8,768]{2,1,0:T(8,128)(2,1)}, u32[]{:S(2)}, u32[]{:S(2)}) async-start(bf16[32,8,768]{2,1,0:T(8,128)(2,1)} %reshape.126), calls=%async_computation | async-start | bytes 786432 | tf_op jit(solution)/shard_map/all_to_all | solution.py:126
  84.9 0.0 copy-done.3
  84.9 0.0 copy-start.4
  84.9 5.4 %fusion.34 = f32[16,3,128,256]{3,2,1,0:T(8,128)} fusion(bf16[16,3,144,128]{3,0,1,2:T(8,128)(2,1)} %convert_bitcast_fusion.3, bf16[18,144,256]{2,1,0:T(8,128)(2,1)S(1)} %get-tuple-element.17), kind=kOutput, calls=%fused_computation.40 | convolution fusion | flops 452984832 | bytes 9240576 | tf_op jit(solution)/shard_map/lqo,lkqb->klbo/dot_general | solution.py:137
  90.4 5.2 %fusion.32 = f32[16,3,128,256]{3,2,1,0:T(8,128)} fusion(bf16[16,3,144,128]{3,0,1,2:T(8,128)(2,1)S(1)} %copy-done.4, bf16[18,144,256]{2,1,0:T(8,128)(2,1)} %copy-done.3), kind=kOutput, calls=%fused_computation.38 | convolution fusion | flops 452984832 | bytes 9240576 | tf_op jit(solution)/shard_map/lqo,lkqb->klbo/dot_general | solution.py:137
  95.6 0.0 copy-done.2
  95.6 7.7 %fusion.29 = bf16[256,16,128]{0,2,1:T(8,128)(2,1)S(1)} fusion(bf16[256,16,128]{0,2,1:T(8,128)(2,1)S(1)} %copy-done.2, f32[16,3,128,256]{3,2,1,0:T(8,128)} %fusion.34, f32[16,3,128,256]{3,2,1,0:T(8,128)} %fusion.32, bf16[16,3,144,128]{3,0,1,2:T(8,128)(2,1)} %convert_bitcast_fusion.1, bf16[18,144,256]{2,1,0:T(8,128)(2,1)} %copy-done.3, ...), kind=kOutput, calls=%fused_computation.36 | convolution fusion | flops 1264582656 | bytes 18022400 | tf_op jit(solution)/shard_map/okc,klbo->lbc/dot_general | solution.py:143
  103.2 1.8 %copy.51 = bf16[256,16,128]{2,1,0:T(8,128)(2,1)} copy(bf16[256,16,128]{0,2,1:T(8,128)(2,1)S(1)} %fusion.29) | data formatting | bytes 2097152
  105.0 0.0 all-to-all-done
  105.0 1.1 reduce_sum.21
  106.1 0.7 broadcast_in_dim.8
  106.8 9.8 %all-to-all-start.1 = ((bf16[16,8,768]{2,1,0:T(8,128)(2,1)}), bf16[16,8,768]{2,1,0:T(8,128)(2,1)S(1)}, u32[]{:S(2)}, u32[]{:S(2)}) async-start(bf16[16,8,768]{2,1,0:T(8,128)(2,1)} %broadcast_in_dim.8), calls=%async_computation.1 | async-start | bytes 393216 | tf_op jit(solution)/shard_map/all_to_all | solution.py:128
  116.6 2.7 %fusion.80 = bf16[256,16,128]{0,2,1:T(8,128)(2,1)S(1)} fusion(f32[18,144,256]{2,1,0:T(8,128)} %get-tuple-element.18, f32[18,144,256]{2,1,0:T(8,128)} %get-tuple-element.19, bf16[256,16,128]{0,2,1:T(8,128)(2,1)S(1)} %copy.34), kind=kLoop, calls=%fused_computation.81 | loop fusion | flops 2097152 | bytes 6291456 | tf_op jit(solution)/shard_map/transpose | solution.py:147
  119.3 1.8 %copy.50 = bf16[256,16,128]{2,1,0:T(8,128)(2,1)} copy(bf16[256,16,128]{0,2,1:T(8,128)(2,1)S(1)} %fusion.80) | data formatting | bytes 2097152
  121.1 5.0 %all-to-all-done.1 = bf16[16,8,768]{2,1,0:T(8,128)(2,1)S(1)} async-done(((bf16[16,8,768]{2,1,0:T(8,128)(2,1)}), bf16[16,8,768]{2,1,0:T(8,128)(2,1)S(1)}, u32[]{:S(2)}, u32[]{:S(2)}) %all-to-all-start.1) | async-done | bytes 196640 | tf_op jit(solution)/shard_map/all_to_all | solution.py:128
  126.1 0.6 convert_reduce_fusion
  (23 shorter events, 0.3 us)
Async XLA Ops:
  0.6 58.5 %copy-start = (bf16[256,3,256]{2,0,1:T(8,128)(2,1)S(1)}, bf16[256,3,256]{2,0,1:T(8,128)(2,1)}, u32[]{:S(2)}) copy-start(bf16[256,3,256]{2,0,1:T(8,128)(2,1)} %param.10) | copy-start | bytes 1179652
  0.6 2.5 %copy-start.7 = (bf16[256,16,128]{2,1,0:T(8,128)(2,1)S(1)}, bf16[256,16,128]{2,1,0:T(8,128)(2,1)}, u32[]{:S(2)}) copy-start(bf16[256,16,128]{2,1,0:T(8,128)(2,1)} %param.7) | copy-start | bytes 3145732
  0.7 15.5 %copy-start.10 = (s32[16,2]{0,1:T(2,128)S(1)}, s32[16,2]{0,1:T(2,128)}, u32[]{:S(2)}) copy-start(s32[16,2]{0,1:T(2,128)} %param.9) | copy-start | bytes 388
  3.9 18.4 %copy-start.1 = (bf16[256,16,128]{0,2,1:T(8,128)(2,1)}, bf16[256,16,128]{0,2,1:T(8,128)(2,1)S(1)}, u32[]{:S(2)}) copy-start(bf16[256,16,128]{0,2,1:T(8,128)(2,1)S(1)} %copy.35) | copy-start | bytes 3145732
  5.4 11.9 %collective-permute-start = (bf16[16,24,256]{2,1,0:T(8,128)(2,1)S(1)}, bf16[16,24,256]{2,1,0:T(8,128)(2,1)S(1)}, u32[]{:S(2)}, u32[]{:S(2)}) collective-permute-start(bf16[16,24,256]{2,1,0:T(8,128)(2,1)S(1)} %get-tuple-element.34), channel_id=1, source_target_pairs={{0,16},{16,0},{32,48},{48,32},{64,80},{80,64},{96,112},{112,96},{1... | collective-permute-start | bytes 589832 | tf_op jit(solution)/shard_map/ppermute | solution.py:21
  14.2 7.1 %collective-permute-start.1 = (bf16[16,24,256]{2,1,0:T(8,128)(2,1)S(1)}, bf16[16,24,256]{2,1,0:T(8,128)(2,1)}, u32[]{:S(2)}, u32[]{:S(2)}) collective-permute-start(bf16[16,24,256]{2,1,0:T(8,128)(2,1)S(1)} %get-tuple-element.35), channel_id=1, source_target_pairs={{16,32},{32,16},{48,64},{64,48},{80,96},{96,80},{112,128},{128,112... | collective-permute-start | bytes 589832 | tf_op jit(solution)/shard_map/ppermute | solution.py:22
  22.3 4.7 %copy-start.9 = (bf16[16,8,256]{2,1,0:T(8,128)(2,1)}, bf16[16,8,256]{2,1,0:T(8,128)(2,1)S(1)}, u32[]{:S(2)}) copy-start(bf16[16,8,256]{2,1,0:T(8,128)(2,1)S(1)} %slice.153) | copy-start | bytes 196612
  22.5 6.9 %collective-permute-start.2 = (bf16[480,256]{1,0:T(8,128)(2,1)S(1)}, bf16[480,256]{1,0:T(8,128)(2,1)S(1)}, u32[]{:S(2)}, u32[]{:S(2)}) collective-permute-start(bf16[480,256]{1,0:T(8,128)(2,1)S(1)} %get-tuple-element.30), channel_id=1, source_target_pairs={{0,1},{1,0},{2,3},{3,2},{4,5},{5,4},{6,7},{7,6},{8,9},{9,8},{10,11... | collective-permute-start | bytes 737288 | tf_op jit(solution)/shard_map/ppermute | solution.py:21
  24.4 5.0 %collective-permute-start.3 = (bf16[480,256]{1,0:T(8,128)(2,1)S(1)}, bf16[480,256]{1,0:T(8,128)(2,1)S(1)}, u32[]{:S(2)}, u32[]{:S(2)}) collective-permute-start(bf16[480,256]{1,0:T(8,128)(2,1)S(1)} %get-tuple-element.31), channel_id=1, source_target_pairs={{1,2},{2,1},{3,4},{4,3},{5,6},{6,5},{7,8},{8,7},{9,10},{10,9},{11,... | collective-permute-start | bytes 737288 | tf_op jit(solution)/shard_map/ppermute | solution.py:22
  43.6 2.6 %copy-start.5 = (bf16[18,3,160,144]{2,0,1,3:T(8,128)(2,1)S(1)}, bf16[18,3,160,144]{2,0,1,3:T(8,128)(2,1)}, u32[]{:S(2)}) copy-start(bf16[18,3,160,144]{2,0,1,3:T(8,128)(2,1)} %get-tuple-element.16) | copy-start | bytes 7464964
  43.7 2.6 %copy-start.8 = (bf16[320,256]{1,0:T(8,128)(2,1)S(1)}, bf16[320,256]{1,0:T(8,128)(2,1)}, u32[]{:S(2)}) copy-start(bf16[320,256]{1,0:T(8,128)(2,1)} %slice.161) | copy-start | bytes 491524
  50.5 8.6 %copy-start.11 = (f32[256]{0:T(256)S(1)}, f32[256]{0:T(256)}, u32[]{:S(2)}) copy-start(f32[256]{0:T(256)} %param.11) | copy-start | bytes 3076
  59.2 7.3 %copy-start.6 = (bf16[3,18,144,256]{3,2,0,1:T(8,128)(2,1)S(1)}, bf16[3,18,144,256]{3,2,0,1:T(8,128)(2,1)}, u32[]{:S(2)}) copy-start(bf16[3,18,144,256]{3,2,0,1:T(8,128)(2,1)} %fusion) | copy-start | bytes 11943940
  66.5 18.4 %copy-start.3 = (bf16[18,144,256]{2,1,0:T(8,128)(2,1)}, bf16[18,144,256]{2,1,0:T(8,128)(2,1)S(1)}, u32[]{:S(2)}) copy-start(bf16[18,144,256]{2,1,0:T(8,128)(2,1)S(1)} %get-tuple-element.17) | copy-start | bytes 3981316
  69.1 36.0 %all-to-all-start = ((bf16[32,8,768]{2,1,0:T(8,128)(2,1)}), bf16[32,8,768]{2,1,0:T(8,128)(2,1)}, u32[]{:S(2)}, u32[]{:S(2)}) async-start(bf16[32,8,768]{2,1,0:T(8,128)(2,1)} %reshape.126), calls=%async_computation | async-start | bytes 786432 | tf_op jit(solution)/shard_map/all_to_all | solution.py:126
  84.9 5.4 %copy-start.4 = (bf16[16,3,144,128]{3,0,1,2:T(8,128)(2,1)S(1)}, bf16[16,3,144,128]{3,0,1,2:T(8,128)(2,1)}, u32[]{:S(2)}) copy-start(bf16[16,3,144,128]{3,0,1,2:T(8,128)(2,1)} %convert_bitcast_fusion.2) | copy-start | bytes 5308420
  90.4 5.2 %copy-start.2 = (bf16[256,16,128]{0,2,1:T(8,128)(2,1)S(1)}, bf16[256,16,128]{0,2,1:T(8,128)(2,1)}, u32[]{:S(2)}) copy-start(bf16[256,16,128]{0,2,1:T(8,128)(2,1)} %copy-done.1) | copy-start | bytes 3145732
  106.8 19.3 %all-to-all-start.1 = ((bf16[16,8,768]{2,1,0:T(8,128)(2,1)}), bf16[16,8,768]{2,1,0:T(8,128)(2,1)S(1)}, u32[]{:S(2)}, u32[]{:S(2)}) async-start(bf16[16,8,768]{2,1,0:T(8,128)(2,1)} %broadcast_in_dim.8), calls=%async_computation.1 | async-start | bytes 393216 | tf_op jit(solution)/shard_map/all_to_all | solution.py:128

commit v2 on v0

v2 whole, which is shorter than its diff:
```python
import math

import jax
import jax.numpy as jnp
from jax import lax
from jax.experimental import pallas as pl
from jax.experimental.pallas import tpu as pltpu
from jax.sharding import PartitionSpec as P

K = 3
SMAX = 8
TAPS = 2 * SMAX + 1

CELL = 256
ROWS = 16
COLS = 128
TALL = ROWS + 2
WIDE = COLS + 2 * SMAX
LINES = 2 * COLS + 4 * 2 * SMAX + COLS + 2 * SMAX + 16
F32, BF16 = jnp.float32, jnp.bfloat16


def gelu_pair(pre):
    root = 0.7978845608028654
    inner = root * (pre + 0.044715 * pre * pre * pre)
    tanh_v = jnp.tanh(inner)
    value = 0.5 * pre * (1.0 + tanh_v)
    slope = 0.5 * (1.0 + tanh_v) + 0.5 * pre * (1.0 - tanh_v * tanh_v) * root * (
        1.0 + 3.0 * 0.044715 * pre * pre
    )
    return (value, slope)


def toeplitz(line):
    return pltpu.roll(
        jnp.broadcast_to(line, (COLS, COLS)), COLS - SMAX, axis=1, stride=1, stride_axis=0
    )


def halves(cyclic, low):
    first, last = cyclic[:SMAX], cyclic[COLS - SMAX :]
    return (
        jnp.where(low, first, 0.0),
        jnp.where(low, 0.0, first),
        jnp.where(low, last, 0.0),
        jnp.where(low, 0.0, last),
    )


def dot(a, b):
    return jnp.dot(a, b, preferred_element_type=F32)


def rows_of(start, count):
    return pl.ds(pl.multiple_of(start, 16), count)


def forward_kernel(
    odd_ref, near, far, field, field_side, cot, cot_side, taps, mix, bias, scale_ref,
    out, term, grad_main, grad_side, taps_all,
    xm, xs, cm, cs, tap32, band, basis,
):
    def put(block, first_row):
        at = 0
        for ref, size, where in (
            (xm, 2 * COLS, 0 if first_row else TALL * COLS),
            (xs, 4 * 2 * SMAX, 0 if first_row else TALL * 4 * SMAX),
            (cm, COLS, 0 if first_row else (TALL - 1) * COLS),
            (cs, 2 * SMAX, 0 if first_row else (TALL - 1) * 2 * SMAX),
            (taps_all, 16, 0 if first_row else (TALL - 1) * 16),
        ):
            ref[where : where + size, :] = block[at : at + size, :]
            at += size

    @pl.when(odd_ref[0] == 1)
    def _():
        put(near, True)
        put(far, False)

    @pl.when(odd_ref[0] == 0)
    def _():
        put(far, True)
        put(near, False)

    xm[2 * COLS : 2 * COLS + ROWS * COLS, :] = field[...]
    xs[8 * SMAX : 8 * SMAX + ROWS * 4 * SMAX, :] = field_side[...]
    xs[(ROWS + 4) * 4 * SMAX :, :] = jnp.zeros((4 * SMAX, CELL), BF16)
    cm[COLS : COLS + ROWS * COLS, :] = cot[...]
    cs[2 * SMAX : 2 * SMAX + ROWS * 2 * SMAX, :] = cot_side[...]
    taps_all[16 : 16 + ROWS * 16, :] = taps[...]
    tap32[...] = taps_all[:, :COLS].astype(F32)
    grad_side[TALL * 2 * SMAX :, :] = jnp.zeros((5 * 2 * SMAX, CELL), BF16)
    band[...] = jnp.zeros(band.shape, BF16)
    low = lax.broadcasted_iota(jnp.int32, (SMAX, COLS), 1) < COLS // 2
    empty = jnp.zeros((SMAX, COLS), F32)

    def build(row, slot):
        lines = tap32[rows_of(row * 16, 16), :]
        for k in range(K):
            at = k * WIDE
            sides = [empty] * 4
            for r in range(3):
                j = k * 3 + r
                cyclic = toeplitz(lines[j : j + 1, :])
                first_lo, first_hi, last_lo, last_hi = halves(cyclic, low)
                to = slice(r * COLS, (r + 1) * COLS)
                band[slot, at : at + COLS, to] = jnp.concatenate(
                    [first_lo, cyclic[SMAX : COLS - SMAX], last_hi], axis=0
                ).astype(BF16)
                band[slot, at + COLS : at + WIDE, to] = jnp.concatenate(
                    [last_lo, first_hi], axis=0
                ).astype(BF16)
                sides = [
                    have + pltpu.roll(part, 16 + 32 * r, axis=1)
                    for have, part in zip(sides, (first_hi, last_lo, last_hi, first_lo))
                ]
            to = slice(3 * COLS, 4 * COLS)
            band[slot, at : at + 16, to] = jnp.concatenate([sides[0], empty], 0).astype(BF16)
            band[slot, at + COLS - 16 : at + COLS, to] = jnp.concatenate(
                [empty, sides[1]], 0
            ).astype(BF16)
            band[slot, at + COLS : at + WIDE, to] = jnp.concatenate(
                [sides[2], sides[3]], 0
            ).astype(BF16)

    def step(row, carry):
        slot = lax.rem(row, 2)
        build(row, slot)
        cells = jnp.concatenate(
            [xm[rows_of(row * COLS, 3 * COLS), :], xs[rows_of(row * 32, COLS), :]], axis=0
        )
        made = dot(band[slot], cells).astype(BF16)
        wide = jnp.concatenate([made[k * WIDE : (k + 1) * WIDE] for k in range(K)], axis=1)
        pre = dot(wide, mix[...]) + bias[...]
        value, slope = gelu_pair(pre)
        main = rows_of(row * COLS, COLS)
        side = rows_of(row * 16, 16)
        basis[main, :] = wide[:COLS]
        grad_main[main, :] = (cm[main, :].astype(F32) * slope[:COLS]).astype(BF16)
        grad_side[side, :] = (cs[side, :].astype(F32) * slope[COLS:]).astype(BF16)

        @pl.when(jnp.logical_and(row > 0, row < TALL - 1))
        def _():
            out[rows_of((row - 1) * COLS, COLS), :] = (
                xm[rows_of((row + 1) * COLS, COLS), :].astype(F32) + value[:COLS]
            ).astype(BF16)

        return carry

    lax.fori_loop(0, TALL, step, 0)
    total = lax.dot_general(
        grad_main[COLS : COLS + ROWS * COLS, :],
        basis[COLS : COLS + ROWS * COLS, :],
        (((0,), (0,)), ((), ())),
        preferred_element_type=F32,
    )
    term[...] = (total * scale_ref[0]).astype(BF16)


def backward_kernel(grad_main, grad_side, taps_all, mix, cot, out, tap32, band):
    tap32[...] = taps_all[:, COLS:].astype(F32)
    band[...] = jnp.zeros(band.shape, BF16)
    low = lax.broadcasted_iota(jnp.int32, (SMAX, COLS), 1) < COLS // 2
    empty = jnp.zeros((SMAX, COLS), F32)

    def step(row, carry):
        slot = lax.rem(row, 2)
        lines = tap32[rows_of(row * 16, 3 * 16), :]
        for k in range(K):
            at = k * COLS
            sides = [empty] * 2
            for i in range(3):
                j = i * 16 + k * 3 + 2 - i
                cyclic = toeplitz(lines[j : j + 1, :])
                first_lo, first_hi, last_lo, last_hi = halves(cyclic, low)
                band[slot, at : at + COLS, i * COLS : (i + 1) * COLS] = jnp.concatenate(
                    [first_lo, cyclic[SMAX : COLS - SMAX], last_hi], axis=0
                ).astype(BF16)
                sides = [
                    have + pltpu.roll(part, 8 + 16 * i, axis=1)
                    for have, part in zip(sides, (first_hi, last_lo))
                ]
            to = slice(3 * COLS, 4 * COLS)
            band[slot, at : at + 16, to] = jnp.concatenate([sides[0], empty], 0).astype(BF16)
            band[slot, at + COLS - 16 : at + COLS, to] = jnp.concatenate(
                [empty, sides[1]], 0
            ).astype(BF16)
        cells = jnp.concatenate(
            [grad_main[rows_of(row * COLS, 3 * COLS), :], grad_side[rows_of(row * 16, COLS), :]],
            axis=0,
        )
        spread = dot(band[slot], cells).astype(BF16)
        wide = jnp.concatenate([spread[k * COLS : (k + 1) * COLS] for k in range(K)], axis=1)
        main = rows_of(row * COLS, COLS)
        out[main, :] = (cot[main, :].astype(F32) + dot(wide, mix[...])).astype(BF16)
        return carry

    lax.fori_loop(0, ROWS, step, 0)


VMEM = pl.BlockSpec(memory_space=pltpu.VMEM)
SMEM = pl.BlockSpec(memory_space=pltpu.SMEM)


def shape(*sizes):
    return jax.ShapeDtypeStruct(sizes, BF16)


def forward(*operands):
    return pl.pallas_call(
        forward_kernel,
        out_shape=(
            shape(ROWS * COLS, CELL),
            shape(CELL, K * CELL),
            shape(TALL * COLS, CELL),
            shape((TALL + 5) * 16, CELL),
            shape(TALL * 16, CELL),
        ),
        in_specs=[SMEM] + [VMEM] * 9 + [SMEM],
        out_specs=(VMEM,) * 5,
        scratch_shapes=[
            pltpu.VMEM(((ROWS + 4) * COLS, CELL), BF16),
            pltpu.VMEM(((ROWS + 5) * 32, CELL), BF16),
            pltpu.VMEM((TALL * COLS, CELL), BF16),
            pltpu.VMEM((TALL * 16, CELL), BF16),
            pltpu.VMEM((TALL * 16, COLS), F32),
            pltpu.VMEM((2, K * WIDE, 4 * COLS), BF16),
            pltpu.VMEM((TALL * COLS, K * CELL), BF16),
        ],
        compiler_params=pltpu.CompilerParams(vmem_limit_bytes=40 * 2**20),
        cost_estimate=pl.CostEstimate(
            flops=5 * 10**9, bytes_accessed=8 * 10**6, transcendentals=600000
        ),
        name="forward",
    )(*operands)


def backward(*operands):
    return pl.pallas_call(
        backward_kernel,
        out_shape=shape(ROWS * COLS, CELL),
        in_specs=[VMEM] * 5,
        out_specs=VMEM,
        scratch_shapes=[
            pltpu.VMEM((TALL * 16, COLS), F32),
            pltpu.VMEM((2, K * COLS, 4 * COLS), BF16),
        ],
        compiler_params=pltpu.CompilerParams(vmem_limit_bytes=40 * 2**20),
        cost_estimate=pl.CostEstimate(
            flops=3 * 10**9, bytes_accessed=5 * 10**6, transcendentals=0
        ),
        name="backward",
    )(*operands)


def swap_pairs(first, last, axis, closed):
    count = lax.axis_size(axis)
    odd = lax.axis_index(axis) % 2 == 1
    near = [(j, j ^ 1) for j in range(count)]
    far = []
    for j in range(1, count, 2):
        if closed or j + 1 < count:
            far += [(j, (j + 1) % count), ((j + 1) % count, j)]
    got_near = lax.ppermute(jnp.where(odd, first, last), axis, near)
    got_far = lax.ppermute(jnp.where(odd, last, first), axis, far)
    return odd, got_near, got_far


def body(field, cotangent, filters, reach, mixing, bias):
    chans, rows, cols = field.shape
    total_rows = rows * lax.axis_size("lat")
    total_cols = cols * lax.axis_size("lon")
    n_lon, n_lat = lax.axis_size("lon"), lax.axis_size("lat")
    offsets = jnp.arange(TAPS, dtype=jnp.int32) - SMAX
    inside = (reach[:, 0:1] <= offsets[None, :]) & (offsets[None, :] <= reach[:, 1:2])
    coef = filters * inside[None, :, None, :].astype(BF16)
    lines = jnp.transpose(coef, (1, 0, 2, 3)).reshape(rows, K * 3, TAPS)
    lines = jnp.pad(lines, ((0, 0), (0, 16 - K * 3), (0, COLS - TAPS)))
    back = jnp.transpose(coef[..., ::-1], (1, 0, 2, 3)).reshape(rows, K * 3, TAPS)
    back = jnp.pad(back, ((0, 0), (0, 16 - K * 3), (0, COLS - TAPS)))
    taps = jnp.concatenate([lines, back], axis=2)

    field_t = jnp.transpose(field, (1, 2, 0))
    cot_t = jnp.transpose(cotangent, (1, 2, 0))
    two, one = 2 * SMAX, SMAX
    odd, near, far = swap_pairs(
        jnp.concatenate([field_t[:, :two], cot_t[:, :one]], axis=1),
        jnp.concatenate([field_t[:, cols - two :], cot_t[:, cols - one :]], axis=1),
        "lon",
        True,
    )
    left, right = jnp.where(odd, near, far), jnp.where(odd, far, near)
    field_side = jnp.concatenate([left[:, :two], right[:, :two]], axis=1)
    cot_side = jnp.concatenate([left[:, two:], right[:, two:]], axis=1)

    def message(two_rows, row):
        return jnp.concatenate(
            [
                field_t[two_rows].reshape(2 * cols, chans),
                field_side[two_rows].reshape(4 * two, chans),
                cot_t[row],
                cot_side[row],
                taps[row],
            ],
            axis=0,
        )

    odd, near, far = swap_pairs(
        message(slice(0, 2), 0), message(slice(rows - 2, rows), rows - 1), "lat", False
    )
    scale = 1.0 / math.sqrt(total_rows * total_cols)
    cot_lines = cot_t.reshape(rows * cols, chans)
    out_t, term, grad_main, grad_side, taps_all = forward(
        odd.astype(jnp.int32).reshape(1),
        near,
        far,
        field_t.reshape(rows * cols, chans),
        field_side.reshape(rows * 2 * two, chans),
        cot_lines,
        cot_side.reshape(rows * two, chans),
        taps.reshape(rows * 16, chans),
        jnp.transpose(mixing, (1, 2, 0)).reshape(K * chans, chans),
        bias.reshape(1, chans),
        jnp.full((1,), scale, F32),
    )
    share = chans // n_lon
    got = lax.all_to_all(term.reshape(n_lon, share, K * chans), "lon", 0, 0)
    part = jnp.sum(got.astype(F32), axis=0).astype(BF16)
    got = lax.all_to_all(jnp.broadcast_to(part[None], (n_lat, share, K * chans)), "lat", 0, 0)
    grad_mixing = jnp.sum(got.astype(F32), axis=0).reshape(share, K, chans)
    grad_t = backward(
        grad_main,
        grad_side,
        taps_all,
        jnp.transpose(mixing, (1, 0, 2)).reshape(K * chans, chans),
        cot_lines,
    )
    return (
        jnp.transpose(out_t.reshape(rows, cols, chans), (2, 0, 1)),
        jnp.transpose(grad_t.reshape(rows, cols, chans), (2, 0, 1)),
        grad_mixing,
    )


def solution(mesh):
    placed = (
        P(None, "lat", "lon"),
        P(None, "lat", "lon"),
        P(None, "lat", None, None),
        P("lat", None),
        P(),
        P(),
    )
    return jax.shard_map(
        body,
        mesh=mesh,
        in_specs=placed,
        out_specs=(P(None, "lat", "lon"), P(None, "lat", "lon"), P("lon", None, None)),
        check_vma=False,
    )
```

time: 363 us -> 105 us (0.29)
  waiting for transfers between devices: 263 us -> 6.73 us
  matrix products: 29 us -> 0 us
  Pallas kernels: 0 us -> 22.8 us
  blocking collectives: 0 us -> 20.6 us
  between operations: 14.3 us -> 1.03 us
  starting transfers between devices: 38.6 us -> 31.4 us
    psum x1 -> x0, waiting for transfers between devices: 262 us -> none  [body(): lax.psum(jnp.einsum('olq,kclq->okc', grad_pre, basis, preferred_element_t...]
    dot_general x13 -> x0, matrix products: 29 us -> none  [the longest x3 9.82 us: body(): jnp.einsum('kclp,lkpq->clq', back_pad[:, :, low:low + rows], mirror_band,...]
    pallas_call x0 -> x2, Pallas kernels: none -> 22.8 us  [the longest x1 13.5 us: forward(): pl.pallas_call(forward_kernel, out_shape=(shape(ROWS * COLS, CELL), shape...]
    all_to_all x0 -> x1, blocking collectives: none -> 20.6 us  [body(): got = lax.all_to_all(term.reshape(n_lon, share, K * chans), 'lon', 0, 0)]
    ppermute x10 -> x4, starting transfers between devices: 38.5 us -> 22.3 us  [the longest x2 17.1 us: swap_pairs(): got_near = lax.ppermute(jnp.where(odd, first, last), axis, near)]
    all_to_all x0 -> x1, starting transfers between devices: none -> 9.14 us  [body(): lax.all_to_all(jnp.broadcast_to(part[None], (n_lat, share, K * chans)), '...]
    ppermute x10 -> x4, waiting for transfers between devices: 0.94 us -> 6.73 us  [the longest x2 6.72 us: swap_pairs(): got_near = lax.ppermute(jnp.where(odd, first, last), axis, near)]
    unnamed x26 -> x44, local copies, waits for them, and re-layouts: 9.94 us -> 13.2 us
  transfers between devices with their start and end apart: 11 -> 5, of which waited for: 2 -> 2; matrix products, arithmetic and copies ran while one was open for 8% -> 5% of each run, Pallas kernels for 0% -> 9%
where the time goes in v2:
time: 105 us
  starting transfers between devices  31.4 us (30%)
  Pallas kernels  22.8 us (22%)
  blocking collectives  20.6 us (20%)
  local copies, waits for them, and re-layouts  18.6 us (18%)
  waiting for transfers between devices  6.73 us (6%)
  other arithmetic  3.6 us (3%)
    all_to_all x1, blocking collectives, body(): got = lax.all_to_all(term.reshape(n_lon, share, K * chans), 'lon', 0, 0)  20.6 us
    ppermute x2, starting transfers between devices, swap_pairs(): got_near = lax.ppermute(jnp.where(odd, first, last), axis, near)  17.1 us
    pallas_call x1, Pallas kernels, forward(): pl.pallas_call(forward_kernel, out_shape=(shape(ROWS * COLS, CELL), shape...  13.5 us
    unnamed x44, local copies, waits for them, and re-layouts  13.2 us
    pallas_call x1, Pallas kernels, backward(): pl.pallas_call(backward_kernel, out_shape=shape(ROWS * COLS, CELL), in_sp...  9.27 us
    all_to_all x1, starting transfers between devices, body(): lax.all_to_all(jnp.broadcast_to(part[None], (n_lat, share, K * chans)), '...  9.14 us
    ppermute x2, waiting for transfers between devices, swap_pairs(): got_near = lax.ppermute(jnp.where(odd, first, last), axis, near)  6.72 us
    ppermute x2, starting transfers between devices, swap_pairs(): got_far = lax.ppermute(jnp.where(odd, last, first), axis, far)  5.17 us
  transfers between devices with their start and end apart: 5, of which 2 were waited for; matrix products, arithmetic and copies ran while one was open for 5% of the time, Pallas kernels for 9%

profile of v2, /device:TPU:1, one launch (start us, length us, event | category | flops | bytes accessed | tf_op | source)
XLA Modules:
  0.0 104.7 jit_solution(17486281498724111960)
XLA Ops:
  0.6 0.0 copy-start.15
  0.7 1.7 %copy.23 = bf16[256,16,128]{0,2,1:T(8,128)(2,1)S(1)} copy(bf16[256,16,128]{2,1,0:T(8,128)(2,1)} %param.6) | data formatting | bytes 2097152 | tf_op args[0]
  2.4 0.0 copy-done.15
  2.4 0.8 copy.24
  3.2 0.0 copy-start.18
  3.2 0.0 copy-start.17
  3.3 0.1 broadcast_select_fusion.4
  3.4 4.5 %collective-permute-start.1 = (bf16[16,24,256]{2,1,0:T(8,128)(2,1)S(1)}, bf16[16,24,256]{2,1,0:T(8,128)(2,1)S(1)}, u32[]{:S(2)}, u32[]{:S(2)}) collective-permute-start(bf16[16,24,256]{2,1,0:T(8,128)(2,1)S(1)} %get-tuple-element.25), channel_id=1, source_target_pairs={{16,32},{32,16},{48,64},{64,48},{80,96},{96,80},{112,128},{128,112... | collective-permute-start | bytes 589832 | tf_op jit(solution)/shard_map/ppermute | solution.py:265
  7.9 11.5 %collective-permute-start = (bf16[16,24,256]{2,1,0:T(8,128)(2,1)S(1)}, bf16[16,24,256]{2,1,0:T(8,128)(2,1)S(1)}, u32[]{:S(2)}, u32[]{:S(2)}) collective-permute-start(bf16[16,24,256]{2,1,0:T(8,128)(2,1)S(1)} %get-tuple-element.26), channel_id=1, source_target_pairs={{0,16},{16,0},{32,48},{48,32},{64,80},{80,64},{96,112},{112,96},{1... | collective-permute-start | bytes 589832 | tf_op jit(solution)/shard_map/ppermute | solution.py:264
  19.4 0.0 copy-done.18
  19.5 0.1 and_convert_fusion
  19.5 0.0 copy-done.17
  19.5 0.1 rev.3
  19.8 0.0 copy-start.2
  19.8 0.0 collective-permute-done.1
  19.8 0.6 collective-permute-done
  20.5 0.0 copy-start
  20.5 0.0 copy-start.16
  20.6 0.0 copy-done.2
  20.6 0.0 copy-start.8
  20.6 0.8 broadcast_select_fusion
  21.5 0.0 copy-done.16
  21.5 0.7 collective-permute-start.3
  22.1 5.6 %collective-permute-start.2 = (bf16[480,256]{1,0:T(8,128)(2,1)}, bf16[480,256]{1,0:T(8,128)(2,1)S(1)}, u32[]{:S(2)}, u32[]{:S(2)}) collective-permute-start(bf16[480,256]{1,0:T(8,128)(2,1)} %get-tuple-element.22), channel_id=1, source_target_pairs={{0,1},{1,0},{2,3},{3,2},{4,5},{5,4},{6,7},{7,6},{8,9},{9,8},{10,11... | collective-permute-start | bytes 737288 | tf_op jit(solution)/shard_map/ppermute | solution.py:264
  27.8 0.0 copy-done
  27.8 0.9 copy.27
  28.7 0.8 pad_maximum_fusion.3
  29.6 0.0 collective-permute-done.3.far
  29.6 0.0 copy-start.4
  29.6 0.7 copy-done.4
  30.3 6.1 %collective-permute-done.2.near = bf16[480,256]{1,0:T(8,128)(2,1)S(1)} collective-permute-done((bf16[480,256]{1,0:T(8,128)(2,1)}, bf16[480,256]{1,0:T(8,128)(2,1)S(1)}, u32[]{:S(2)}, u32[]{:S(2)}) %collective-permute-start.2) | collective-permute-done | bytes 245792 | tf_op jit(solution)/shard_map/ppermute | solution.py:264
  36.4 0.0 copy-start.6
  36.4 0.7 copy-done.6
  37.1 0.0 copy-done.8
  37.1 0.0 copy-start.1
  37.1 1.0 copy-done.1
  38.1 0.0 copy-start.3
  38.1 0.9 copy-done.3
  39.0 0.0 copy-start.5
  39.0 0.9 copy-done.5
  39.9 0.0 copy-start.7
  39.9 0.9 copy-done.7
  40.9 13.5 %forward.1 = (bf16[2048,256]{1,0:T(8,128)(2,1)S(1)}, bf16[256,768]{1,0:T(8,128)(2,1)S(1)}, bf16[2304,256]{1,0:T(8,128)(2,1)S(1)}, bf16[368,256]{1,0:T(8,128)(2,1)S(1)}, bf16[288,256]{1,0:T(8,128)(2,1)S(1)}) custom-call(s32[1]{0:T(128)} %bitcast.odd_ref, bf16[480,256]{1,0:T(8,128)(2,1)S(1)} %copy-done.7, bf16[480,256]{1,0:T(8,128)(2,1)S(1)} %copy-done.5, ...), custom_call_target="tpu_custom_call" | custom-call | flops 5000000000 | bytes 8000000 | tf_op jit(solution)/shard_map/forward/pallas_call | solution.py:210
  54.4 0.0 copy-start.9
  54.4 1.0 copy-done.9
  55.4 0.0 copy-start.11
  55.4 0.7 copy-done.11
  56.0 0.0 copy-start.13
  56.0 0.7 copy-done.13
  56.7 20.6 %all_to_all.10 = bf16[32,8,768]{2,1,0:T(8,128)(2,1)S(1)} all-to-all(bf16[32,8,768]{2,1,0:T(8,128)(2,1)S(1)} %bitcast.68), channel_id=1, replica_groups=mesh['lon'=32,'lat'=16] {'lon'}, dimensions={0} | all-to-all | bytes 786432 | tf_op jit(solution)/shard_map/all_to_all | solution.py:327
  77.3 0.1 reduce_sum.21
  77.4 0.7 broadcast_in_dim.2
  78.1 9.1 %all-to-all-start.1 = ((bf16[16,8,768]{2,1,0:T(8,128)(2,1)}), bf16[16,8,768]{2,1,0:T(8,128)(2,1)}, u32[]{:S(2)}, u32[]{:S(2)}) async-start(bf16[16,8,768]{2,1,0:T(8,128)(2,1)} %broadcast_in_dim.2), calls=%async_computation.1 | async-start | bytes 393216 | tf_op jit(solution)/shard_map/all_to_all | solution.py:329
  87.2 1.8 %copy.28 = bf16[16,128,256]{1,0,2:T(8,128)(2,1)} copy(bf16[16,128,256]{2,1,0:T(8,128)(2,1)S(1)} %bitcast.63) | data formatting | bytes 2097152 | tf_op jit(solution)/shard_map/reshape | solution.py:339
  89.0 0.0 copy-start.10
  89.0 1.3 %copy-done.10 = bf16[2304,256]{1,0:T(8,128)(2,1)S(1)} copy-done((bf16[2304,256]{1,0:T(8,128)(2,1)S(1)}, bf16[2304,256]{1,0:T(8,128)(2,1)}, u32[]{:S(2)}) %copy-start.10) | copy-done | bytes 1179672
  90.3 0.0 copy-start.12
  90.3 0.9 copy-done.12
  91.2 0.0 copy-start.14
  91.2 0.9 copy-done.14
  92.1 9.3 %backward.1 = bf16[2048,256]{1,0:T(8,128)(2,1)S(1)} custom-call(bf16[2304,256]{1,0:T(8,128)(2,1)S(1)} %copy-done.10, bf16[368,256]{1,0:T(8,128)(2,1)S(1)} %copy-done.12, bf16[288,256]{1,0:T(8,128)(2,1)S(1)} %copy-done.14, bf16[768,256]{1,0:T(8,128)(2,1)S(1)} %bitcast.66, bf16[2048,256]{1,0:T(8,128)(2,1)S(1)} %bitcast.62), custom_call_target="tpu_custom_call" | custom-call | flops 3000000000 | bytes 5000000 | tf_op jit(solution)/shard_map/backward/pallas_call | solution.py:239
  101.4 1.8 %copy.29 = bf16[16,128,256]{1,0,2:T(8,128)(2,1)} copy(bf16[16,128,256]{2,1,0:T(8,128)(2,1)S(1)} %bitcast.64) | data formatting | bytes 2097152 | tf_op jit(solution)/shard_map/reshape | solution.py:340
  103.2 0.0 all-to-all-done.1
  103.2 1.6 %convert_reduce_fusion = f32[8,768]{1,0:T(8,128)} fusion(bf16[16,8,768]{2,1,0:T(8,128)(2,1)} %all-to-all-done.1), kind=kLoop, calls=%fused_computation | loop fusion | flops 190464 | bytes 221184 | tf_op jit(solution)/shard_map/reduce_sum | solution.py:330
  (22 shorter events, 0.3 us)
Async XLA Ops:
  0.6 1.8 %copy-start.15 = (bf16[256,16,128]{2,1,0:T(8,128)(2,1)S(1)}, bf16[256,16,128]{2,1,0:T(8,128)(2,1)}, u32[]{:S(2)}) copy-start(bf16[256,16,128]{2,1,0:T(8,128)(2,1)} %param.7) | copy-start | bytes 3145732
  3.2 16.2 %copy-start.18 = (s32[16,2]{0,1:T(2,128)S(1)}, s32[16,2]{0,1:T(2,128)}, u32[]{:S(2)}) copy-start(s32[16,2]{0,1:T(2,128)} %param.9) | copy-start | bytes 388
  3.2 16.3 %copy-start.17 = (bf16[3,16,3,17]{3,1,2,0:T(8,128)(2,1)S(1)}, bf16[3,16,3,17]{3,1,2,0:T(8,128)(2,1)}, u32[]{:S(2)}) copy-start(bf16[3,16,3,17]{3,1,2,0:T(8,128)(2,1)} %param.8) | copy-start | bytes 14692
  3.4 16.4 %collective-permute-start.1 = (bf16[16,24,256]{2,1,0:T(8,128)(2,1)S(1)}, bf16[16,24,256]{2,1,0:T(8,128)(2,1)S(1)}, u32[]{:S(2)}, u32[]{:S(2)}) collective-permute-start(bf16[16,24,256]{2,1,0:T(8,128)(2,1)S(1)} %get-tuple-element.25), channel_id=1, source_target_pairs={{16,32},{32,16},{48,64},{64,48},{80,96},{96,80},{112,128},{128,112... | collective-permute-start | bytes 589832 | tf_op jit(solution)/shard_map/ppermute | solution.py:265
  7.9 12.5 %collective-permute-start = (bf16[16,24,256]{2,1,0:T(8,128)(2,1)S(1)}, bf16[16,24,256]{2,1,0:T(8,128)(2,1)S(1)}, u32[]{:S(2)}, u32[]{:S(2)}) collective-permute-start(bf16[16,24,256]{2,1,0:T(8,128)(2,1)S(1)} %get-tuple-element.26), channel_id=1, source_target_pairs={{0,16},{16,0},{32,48},{48,32},{64,80},{80,64},{96,112},{112,96},{1... | collective-permute-start | bytes 589832 | tf_op jit(solution)/shard_map/ppermute | solution.py:264
  19.8 0.9 copy-start.2
  20.5 7.3 %copy-start = (bf16[256,3,256]{2,0,1:T(8,128)(2,1)S(1)}, bf16[256,3,256]{2,0,1:T(8,128)(2,1)}, u32[]{:S(2)}) copy-start(bf16[256,3,256]{2,0,1:T(8,128)(2,1)} %param.10) | copy-start | bytes 1179652
  20.5 1.0 copy-start.16
  20.6 16.4 %copy-start.8 = (f32[256]{0:T(256)S(1)}, f32[256]{0:T(256)}, u32[]{:S(2)}) copy-start(f32[256]{0:T(256)} %param.11) | copy-start | bytes 3076
  21.5 8.1 %collective-permute-start.3 = (bf16[480,256]{1,0:T(8,128)(2,1)}, bf16[480,256]{1,0:T(8,128)(2,1)S(1)}, u32[]{:S(2)}, u32[]{:S(2)}) collective-permute-start(bf16[480,256]{1,0:T(8,128)(2,1)} %get-tuple-element.21), channel_id=1, source_target_pairs={{1,2},{2,1},{3,4},{4,3},{5,6},{6,5},{7,8},{8,7},{9,10},{10,9},{11,... | collective-permute-start | bytes 737288 | tf_op jit(solution)/shard_map/ppermute | solution.py:265
  22.1 14.2 %collective-permute-start.2 = (bf16[480,256]{1,0:T(8,128)(2,1)}, bf16[480,256]{1,0:T(8,128)(2,1)S(1)}, u32[]{:S(2)}, u32[]{:S(2)}) collective-permute-start(bf16[480,256]{1,0:T(8,128)(2,1)} %get-tuple-element.22), channel_id=1, source_target_pairs={{0,1},{1,0},{2,3},{3,2},{4,5},{5,4},{6,7},{7,6},{8,9},{9,8},{10,11... | collective-permute-start | bytes 737288 | tf_op jit(solution)/shard_map/ppermute | solution.py:264
  29.6 0.7 copy-start.4
  36.4 0.7 copy-start.6
  37.1 1.0 copy-start.1
  38.1 0.9 copy-start.3
  39.0 0.9 copy-start.5
  39.9 0.9 copy-start.7
  54.4 1.0 copy-start.9
  55.4 0.7 copy-start.11
  56.0 0.7 copy-start.13
  78.1 25.1 %all-to-all-start.1 = ((bf16[16,8,768]{2,1,0:T(8,128)(2,1)}), bf16[16,8,768]{2,1,0:T(8,128)(2,1)}, u32[]{:S(2)}, u32[]{:S(2)}) async-start(bf16[16,8,768]{2,1,0:T(8,128)(2,1)} %broadcast_in_dim.2), calls=%async_computation.1 | async-start | bytes 393216 | tf_op jit(solution)/shard_map/all_to_all | solution.py:329
  89.0 1.3 %copy-start.10 = (bf16[2304,256]{1,0:T(8,128)(2,1)S(1)}, bf16[2304,256]{1,0:T(8,128)(2,1)}, u32[]{:S(2)}) copy-start(bf16[2304,256]{1,0:T(8,128)(2,1)} %copy-done.9) | copy-start | bytes 3538948
  90.3 0.9 copy-start.12
  91.2 0.9 copy-start.14

commit v3 on v2

--- a/solution.py
+++ b/solution.py
@@ -16,6 +16,8 @@
 COLS = 128
 TALL = ROWS + 2
 WIDE = COLS + 2 * SMAX
+PACK = 6
+BACK_PACK = 8
 LINES = 2 * COLS + 4 * 2 * SMAX + COLS + 2 * SMAX + 16
 F32, BF16 = jnp.float32, jnp.bfloat16
 
@@ -56,41 +58,75 @@
 
 
 def forward_kernel(
-    odd_ref, near, far, field, field_side, cot, cot_side, taps, mix, bias, scale_ref,
-    out, term, grad_main, grad_side, taps_all,
-    xm, xs, cm, cs, tap32, band, basis,
+    odd_ref, near, far, field, field_side, cot, cot_side, taps, mix_in, bias, scale_ref,
+    out_hbm, term_hbm, grad_main_hbm, grad_side_hbm, taps_hbm,
+    xm, xs, cm, cs, tap32, band, basis, basis_side, out, term, grad_main, grad_side, taps_all, mix,
+    sem_own, sem_near, sem_far, sem_out,
 ):
-    def put(block, first_row):
-        at = 0
-        for ref, size, where in (
-            (xm, 2 * COLS, 0 if first_row else TALL * COLS),
-            (xs, 4 * 2 * SMAX, 0 if first_row else TALL * 4 * SMAX),
-            (cm, COLS, 0 if first_row else (TALL - 1) * COLS),
-            (cs, 2 * SMAX, 0 if first_row else (TALL - 1) * 2 * SMAX),
-            (taps_all, 16, 0 if first_row else (TALL - 1) * 16),
+    def edges(block, first_row, sems):
+        at, copies = 0, []
+        for i, (ref, size, where) in enumerate(
+            (
+                (xm, 2 * COLS, 0 if first_row else TALL * COLS),
+                (xs, 4 * 2 * SMAX, 0 if first_row else TALL * 4 * SMAX),
+                (cm, COLS, 0 if first_row else (TALL - 1) * COLS),
+                (cs, 2 * SMAX, 0 if first_row else (TALL - 1) * 2 * SMAX),
+                (taps_all, 16, 0 if first_row else (TALL - 1) * 16),
+            )
         ):
-            ref[where : where + size, :] = block[at : at + size, :]
+            copies.append(
+                pltpu.make_async_copy(
+                    block.at[pl.ds(at, size)], ref.at[pl.ds(where, size)], sems.at[i]
+                )
+            )
             at += size
-
-    @pl.when(odd_ref[0] == 1)
+        return copies
+
+    own = [
+        pltpu.make_async_copy(src, dst, sem_own.at[i])
+        for i, (src, dst) in enumerate(
+            (
+                (taps, taps_all.at[pl.ds(16, ROWS * 16)]),
+                (field, xm.at[pl.ds(2 * COLS, ROWS * COLS)]),
+                (field_side, xs.at[pl.ds(8 * SMAX, ROWS * 4 * SMAX)]),
+                (cot, cm.at[pl.ds(COLS, ROWS * COLS)]),
+                (cot_side, cs.at[pl.ds(2 * SMAX, ROWS * 2 * SMAX)]),
+                (mix_in, mix),
+            )
+        )
+    ]
+    odd = odd_ref[0] == 1
+    even = odd_ref[0] == 0
+
+    @pl.when(odd)
     def _():
-        put(near, True)
-        put(far, False)
-
-    @pl.when(odd_ref[0] == 0)
+        for copy in edges(near, True, sem_near) + edges(far, False, sem_far):
+            copy.start()
+
+    @pl.when(even)
     def _():
-        put(far, True)
-        put(near, False)
-
-    xm[2 * COLS : 2 * COLS + ROWS * COLS, :] = field[...]
-    xs[8 * SMAX : 8 * SMAX + ROWS * 4 * SMAX, :] = field_side[...]
+        for copy in edges(far, True, sem_far) + edges(near, False, sem_near):
+            copy.start()
+
+    for copy in own:
+        copy.start()
+    band[...] = jnp.zeros(band.shape, BF16)
     xs[(ROWS + 4) * 4 * SMAX :, :] = jnp.zeros((4 * SMAX, CELL), BF16)
-    cm[COLS : COLS + ROWS * COLS, :] = cot[...]
-    cs[2 * SMAX : 2 * SMAX + ROWS * 2 * SMAX, :] = cot_side[...]
-    taps_all[16 : 16 + ROWS * 16, :] = taps[...]
+
+    @pl.when(odd)
+    def _():
+        for copy in edges(near, True, sem_near) + edges(far, False, sem_far):
+            copy.wait()
+
+    @pl.when(even)
+    def _():
+        for copy in edges(far, True, sem_far) + edges(near, False, sem_near):
+            copy.wait()
+
+    for copy in own:
+        copy.wait()
     tap32[...] = taps_all[:, :COLS].astype(F32)
-    grad_side[TALL * 2 * SMAX :, :] = jnp.zeros((5 * 2 * SMAX, CELL), BF16)
-    band[...] = jnp.zeros(band.shape, BF16)
+    grad_side[TALL * 2 * SMAX :, :] = jnp.zeros((7 * 2 * SMAX, CELL), BF16)
     low = lax.broadcasted_iota(jnp.int32, (SMAX, COLS), 1) < COLS // 2
     empty = jnp.zeros((SMAX, COLS), F32)
 
@@ -123,31 +159,44 @@
                 [sides[2], sides[3]], 0
             ).astype(BF16)
 
-    def step(row, carry):
-        slot = lax.rem(row, 2)
-        build(row, slot)
-        cells = jnp.concatenate(
-            [xm[rows_of(row * COLS, 3 * COLS), :], xs[rows_of(row * 32, COLS), :]], axis=0
+    def step(group, carry):
+        first = group * PACK
+        for i in range(PACK):
+            row = first + i
+            build(row, i)
+            cells = jnp.concatenate(
+                [xm[rows_of(row * COLS, 3 * COLS), :], xs[rows_of(row * 32, COLS), :]], axis=0
+            )
+            made = dot(band[i], cells).astype(BF16)
+            for k in range(K):
+                to = slice(k * CELL, (k + 1) * CELL)
+                basis[rows_of(row * COLS, COLS), to] = made[k * WIDE : k * WIDE + COLS]
+                basis_side[i * 16 : (i + 1) * 16, to] = made[k * WIDE + COLS : (k + 1) * WIDE]
+        main = rows_of(first * COLS, PACK * COLS)
+        side = rows_of(first * 16, PACK * 16)
+        value, slope = gelu_pair(dot(basis[main, :], mix[...]) + bias[...])
+        grad_main[main, :] = (cm[main, :].astype(F32) * slope).astype(BF16)
+        here = xm[rows_of((first + 1) * COLS, PACK * COLS), :].astype(F32)
+        out[main, :] = (here + value).astype(BF16)
+        slope = gelu_pair(dot(basis_side[...], mix[...]) + bias[...])[1]
+        grad_side[side, :] = (cs[side, :].astype(F32) * slope).astype(BF16)
+        return carry
+
+    lax.fori_loop(0, TALL // PACK, step, 0)
+    results = [
+        pltpu.make_async_copy(src, dst, sem_out.at[i])
+        for i, (src, dst) in enumerate(
+            (
+                (out.at[pl.ds(COLS, ROWS * COLS)], out_hbm),
+                (grad_main, grad_main_hbm),
+                (grad_side, grad_side_hbm),
+                (taps_all, taps_hbm),
+                (term, term_hbm),
+            )
         )
-        made = dot(band[slot], cells).astype(BF16)
-        wide = jnp.concatenate([made[k * WIDE : (k + 1) * WIDE] for k in range(K)], axis=1)
-        pre = dot(wide, mix[...]) + bias[...]
-        value, slope = gelu_pair(pre)
-        main = rows_of(row * COLS, COLS)
-        side = rows_of(row * 16, 16)
-        basis[main, :] = wide[:COLS]
-        grad_main[main, :] = (cm[main, :].astype(F32) * slope[:COLS]).astype(BF16)
-        grad_side[side, :] = (cs[side, :].astype(F32) * slope[COLS:]).astype(BF16)
-
-        @pl.when(jnp.logical_and(row > 0, row < TALL - 1))
-        def _():
-            out[rows_of((row - 1) * COLS, COLS), :] = (
-                xm[rows_of((row + 1) * COLS, COLS), :].astype(F32) + value[:COLS]
-            ).astype(BF16)
-
-        return carry
-
-    lax.fori_loop(0, TALL, step, 0)
+    ]
+    for copy in results[:4]:
+        copy.start()
     total = lax.dot_general(
         grad_main[COLS : COLS + ROWS * COLS, :],
         basis[COLS : COLS + ROWS * COLS, :],
@@ -155,16 +204,37 @@
         preferred_element_type=F32,
     )
     term[...] = (total * scale_ref[0]).astype(BF16)
-
-
-def backward_kernel(grad_main, grad_side, taps_all, mix, cot, out, tap32, band):
+    results[4].start()
+    for copy in results:
+        copy.wait()
+
+
+def backward_kernel(
+    grad_main_hbm, grad_side_hbm, taps_hbm, mix_hbm, cot_hbm, out_hbm,
+    tap32, band, spread, grad_main, grad_side, taps_all, mix, cot, out, sem,
+):
+    loads = [
+        pltpu.make_async_copy(src, dst, sem.at[i])
+        for i, (src, dst) in enumerate(
+            (
+                (taps_hbm, taps_all),
+                (grad_main_hbm, grad_main),
+                (grad_side_hbm, grad_side),
+                (mix_hbm, mix),
+                (cot_hbm, cot),
+            )
+        )
+    ]
+    for copy in loads:
+        copy.start()
+    band[...] = jnp.zeros(band.shape, BF16)
+    for copy in loads:
+        copy.wait()
     tap32[...] = taps_all[:, COLS:].astype(F32)
-    band[...] = jnp.zeros(band.shape, BF16)
     low = lax.broadcasted_iota(jnp.int32, (SMAX, COLS), 1) < COLS // 2
     empty = jnp.zeros((SMAX, COLS), F32)
 
-    def step(row, carry):
-        slot = lax.rem(row, 2)
+    def build(row, slot):
         lines = tap32[rows_of(row * 16, 3 * 16), :]
         for k in range(K):
             at = k * COLS
@@ -185,20 +255,36 @@
             band[slot, at + COLS - 16 : at + COLS, to] = jnp.concatenate(
                 [empty, sides[1]], 0
             ).astype(BF16)
-        cells = jnp.concatenate(
-            [grad_main[rows_of(row * COLS, 3 * COLS), :], grad_side[rows_of(row * 16, COLS), :]],
-            axis=0,
-        )
-        spread = dot(band[slot], cells).astype(BF16)
-        wide = jnp.concatenate([spread[k * COLS : (k + 1) * COLS] for k in range(K)], axis=1)
-        main = rows_of(row * COLS, COLS)
-        out[main, :] = (cot[main, :].astype(F32) + dot(wide, mix[...])).astype(BF16)
+
+    def step(group, carry):
+        first = group * BACK_PACK
+        for i in range(BACK_PACK):
+            row = first + i
+            build(row, i)
+            cells = jnp.concatenate(
+                [
+                    grad_main[rows_of(row * COLS, 3 * COLS), :],
+                    grad_side[rows_of(row * 16, COLS), :],
+                ],
+                axis=0,
+            )
+            made = dot(band[i], cells).astype(BF16)
+            for k in range(K):
+                spread[i * COLS : (i + 1) * COLS, k * CELL : (k + 1) * CELL] = made[
+                    k * COLS : (k + 1) * COLS
+                ]
+        main = rows_of(first * COLS, BACK_PACK * COLS)
+        out[main, :] = (cot[main, :].astype(F32) + dot(spread[...], mix[...])).astype(BF16)
         return carry
 
-    lax.fori_loop(0, ROWS, step, 0)
+    lax.fori_loop(0, ROWS // BACK_PACK, step, 0)
+    copy = pltpu.make_async_copy(out, out_hbm, sem.at[5])
+    copy.start()
+    copy.wait()
 
 
 VMEM = pl.BlockSpec(memory_space=pltpu.VMEM)
+HBM = pl.BlockSpec(memory_space=pl.ANY)
 SMEM = pl.BlockSpec(memory_space=pltpu.SMEM)
 
 
@@ -213,21 +299,32 @@
             shape(ROWS * COLS, CELL),
             shape(CELL, K * CELL),
             shape(TALL * COLS, CELL),
-            shape((TALL + 5) * 16, CELL),
+            shape((TALL + 7) * 16, CELL),
             shape(TALL * 16, CELL),
         ),
-        in_specs=[SMEM] + [VMEM] * 9 + [SMEM],
-        out_specs=(VMEM,) * 5,
+        in_specs=[SMEM] + [HBM] * 8 + [VMEM, SMEM],
+        out_specs=(HBM,) * 5,
         scratch_shapes=[
             pltpu.VMEM(((ROWS + 4) * COLS, CELL), BF16),
             pltpu.VMEM(((ROWS + 5) * 32, CELL), BF16),
             pltpu.VMEM((TALL * COLS, CELL), BF16),
             pltpu.VMEM((TALL * 16, CELL), BF16),
             pltpu.VMEM((TALL * 16, COLS), F32),
-            pltpu.VMEM((2, K * WIDE, 4 * COLS), BF16),
+            pltpu.VMEM((PACK, K * WIDE, 4 * COLS), BF16),
             pltpu.VMEM((TALL * COLS, K * CELL), BF16),
+            pltpu.VMEM((PACK * 16, K * CELL), BF16),
+            pltpu.VMEM((TALL * COLS, CELL), BF16),
+            pltpu.VMEM((CELL, K * CELL), BF16),
+            pltpu.VMEM((TALL * COLS, CELL), BF16),
+            pltpu.VMEM(((TALL + 7) * 16, CELL), BF16),
+            pltpu.VMEM((TALL * 16, CELL), BF16),
+            pltpu.VMEM((K * CELL, CELL), BF16),
+            pltpu.SemaphoreType.DMA((6,)),
+            pltpu.SemaphoreType.DMA((5,)),
+            pltpu.SemaphoreType.DMA((5,)),
+            pltpu.SemaphoreType.DMA((5,)),
         ],
-        compiler_params=pltpu.CompilerParams(vmem_limit_bytes=40 * 2**20),
+        compiler_params=pltpu.CompilerParams(vmem_limit_bytes=60 * 2**20),
         cost_estimate=pl.CostEstimate(
             flops=5 * 10**9, bytes_accessed=8 * 10**6, transcendentals=600000
         ),
@@ -239,13 +336,21 @@
     return pl.pallas_call(
         backward_kernel,
         out_shape=shape(ROWS * COLS, CELL),
-        in_specs=[VMEM] * 5,
-        out_specs=VMEM,
+        in_specs=[HBM] * 5,
+        out_specs=HBM,
         scratch_shapes=[
             pltpu.VMEM((TALL * 16, COLS), F32),
-            pltpu.VMEM((2, K * COLS, 4 * COLS), BF16),
+            pltpu.VMEM((BACK_PACK, K * COLS, 4 * COLS), BF16),
+            pltpu.VMEM((BACK_PACK * COLS, K * CELL), BF16),
+            pltpu.VMEM((TALL * COLS, CELL), BF16),
+            pltpu.VMEM(((TALL + 7) * 16, CELL), BF16),
+            pltpu.VMEM((TALL * 16, CELL), BF16),
+            pltpu.VMEM((K * CELL, CELL), BF16),
+            pltpu.VMEM((ROWS * COLS, CELL), BF16),
+            pltpu.VMEM((ROWS * COLS, CELL), BF16),
+            pltpu.SemaphoreType.DMA((6,)),
         ],
-        compiler_params=pltpu.CompilerParams(vmem_limit_bytes=40 * 2**20),
+        compiler_params=pltpu.CompilerParams(vmem_limit_bytes=60 * 2**20),
         cost_estimate=pl.CostEstimate(
             flops=3 * 10**9, bytes_accessed=5 * 10**6, transcendentals=0
         ),
@@ -325,9 +430,6 @@
     )
     share = chans // n_lon
     got = lax.all_to_all(term.reshape(n_lon, share, K * chans), "lon", 0, 0)
-    part = jnp.sum(got.astype(F32), axis=0).astype(BF16)
-    got = lax.all_to_all(jnp.broadcast_to(part[None], (n_lat, share, K * chans)), "lat", 0, 0)
-    grad_mixing = jnp.sum(got.astype(F32), axis=0).reshape(share, K, chans)
     grad_t = backward(
         grad_main,
         grad_side,
@@ -335,6 +437,10 @@
         jnp.transpose(mixing, (1, 0, 2)).reshape(K * chans, chans),
         cot_lines,
     )
+    part = jnp.sum(got.astype(F32), axis=0).astype(BF16)
+    part, grad_t = lax.optimization_barrier((part, grad_t))
+    got = lax.all_to_all(jnp.broadcast_to(part[None], (n_lat, share, K * chans)), "lat", 0, 0)
+    grad_mixing = jnp.sum(got.astype(F32), axis=0).reshape(share, K, chans)
     return (
         jnp.transpose(out_t.reshape(rows, cols, chans), (2, 0, 1)),
         jnp.transpose(grad_t.reshape(rows, cols, chans), (2, 0, 1)),

time: 105 us -> 91 us (0.87)
  blocking collectives: 20.6 us -> 0 us
  waiting for transfers between devices: 6.73 us -> 21.7 us
  local copies, waits for them, and re-layouts: 18.6 us -> 8.69 us
  starting transfers between devices: 31.4 us -> 37 us
  Pallas kernels: 22.8 us -> 19.7 us
  other arithmetic: 3.6 us -> 2.44 us
    all_to_all x1 -> x0, blocking collectives: 20.6 us -> none  [body(): got = lax.all_to_all(term.reshape(n_lon, share, K * chans), 'lon', 0, 0)]
    unnamed x44 -> x28, local copies, waits for them, and re-layouts: 13.2 us -> 3.28 us
    all_to_all x0 -> x1, waiting for transfers between devices: none -> 8.19 us  [body(): got = lax.all_to_all(term.reshape(n_lon, share, K * chans), 'lon', 0, 0)]
    all_to_all x1, waiting for transfers between devices: 0.01 us -> 6.92 us  [body(): lax.all_to_all(jnp.broadcast_to(part[None], (n_lat, share, K * chans)), '...]
    all_to_all x0 -> x1, starting transfers between devices: none -> 5.4 us  [body(): got = lax.all_to_all(term.reshape(n_lon, share, K * chans), 'lon', 0, 0)]
    pallas_call x1, Pallas kernels: 9.27 us -> 7.2 us  [backward(): pl.pallas_call(backward_kernel, out_shape=shape(ROWS * COLS, CELL), in_sp...]
  transfers between devices with their start and end apart: 5 -> 6, of which waited for: 2 -> 4; matrix products, arithmetic and copies ran while one was open for 5% -> 7% of each run, Pallas kernels for 9% -> 8%
where the time goes in v3:
time: 91 us; the launch traced here: 90.5 us
  starting transfers between devices  37 us (41%)
  waiting for transfers between devices  21.7 us (24%)
  Pallas kernels  19.7 us (22%)
  local copies, waits for them, and re-layouts  8.69 us (10%)
  other arithmetic  2.44 us (3%)
  between operations  1.04 us (1%)
    ppermute x2, starting transfers between devices, swap_pairs(): got_near = lax.ppermute(jnp.where(odd, first, last), axis, near)  17.1 us
    pallas_call x1, Pallas kernels, forward(): pl.pallas_call(forward_kernel, out_shape=(shape(ROWS * COLS, CELL), shape...  12.5 us
    all_to_all x1, starting transfers between devices, body(): lax.all_to_all(jnp.broadcast_to(part[None], (n_lat, share, K * chans)), '...  9.32 us
    all_to_all x1, waiting for transfers between devices, body(): got = lax.all_to_all(term.reshape(n_lon, share, K * chans), 'lon', 0, 0)  8.19 us
    pallas_call x1, Pallas kernels, backward(): pl.pallas_call(backward_kernel, out_shape=shape(ROWS * COLS, CELL), in_sp...  7.2 us
    all_to_all x1, waiting for transfers between devices, body(): lax.all_to_all(jnp.broadcast_to(part[None], (n_lat, share, K * chans)), '...  6.92 us
    ppermute x2, waiting for transfers between devices, swap_pairs(): got_near = lax.ppermute(jnp.where(odd, first, last), axis, near)  6.56 us
    all_to_all x1, starting transfers between devices, body(): got = lax.all_to_all(term.reshape(n_lon, share, K * chans), 'lon', 0, 0)  5.4 us
  transfers between devices with their start and end apart: 6, of which 4 were waited for; matrix products, arithmetic and copies ran while one was open for 7% of the time, Pallas kernels for 8%

profile of v3, /device:TPU:1, one launch (start us, length us, event | category | flops | bytes accessed | tf_op | source)
XLA Modules:
  0.0 90.5 jit_solution(3253467867520405851)
XLA Ops:
  0.6 0.0 copy-start.2
  0.7 1.7 %copy.23 = bf16[256,16,128]{0,2,1:T(8,128)(2,1)S(1)} copy(bf16[256,16,128]{2,1,0:T(8,128)(2,1)} %param.6) | data formatting | bytes 2097152 | tf_op args[0]
  2.4 0.0 copy-start
  2.4 0.0 copy-done.2
  2.4 0.8 copy.24
  3.2 0.0 copy-start.1
  3.2 0.0 copy-start.8
  3.3 0.0 copy-start.7
  3.3 0.1 broadcast_select_fusion.4
  3.4 4.5 %collective-permute-start.1 = (bf16[16,24,256]{2,1,0:T(8,128)(2,1)S(1)}, bf16[16,24,256]{2,1,0:T(8,128)(2,1)S(1)}, u32[]{:S(2)}, u32[]{:S(2)}) collective-permute-start(bf16[16,24,256]{2,1,0:T(8,128)(2,1)S(1)} %get-tuple-element.29), channel_id=1, source_target_pairs={{16,32},{32,16},{48,64},{64,48},{80,96},{96,80},{112,128},{128,112... | collective-permute-start | bytes 589832 | tf_op jit(solution)/shard_map/ppermute | solution.py:370
  7.9 11.5 %collective-permute-start = (bf16[16,24,256]{2,1,0:T(8,128)(2,1)S(1)}, bf16[16,24,256]{2,1,0:T(8,128)(2,1)S(1)}, u32[]{:S(2)}, u32[]{:S(2)}) collective-permute-start(bf16[16,24,256]{2,1,0:T(8,128)(2,1)S(1)} %get-tuple-element.30), channel_id=1, source_target_pairs={{0,16},{16,0},{32,48},{48,32},{64,80},{80,64},{96,112},{112,96},{1... | collective-permute-start | bytes 589832 | tf_op jit(solution)/shard_map/ppermute | solution.py:369
  19.4 0.0 copy-done
  19.5 0.0 copy-done.8
  19.5 0.1 and_convert_fusion
  19.6 0.0 copy-done.7
  19.6 0.1 rev.3
  19.8 0.0 copy-start.6
  19.8 0.0 collective-permute-done.1
  19.8 0.6 collective-permute-done
  20.5 0.0 copy-start.5
  20.6 0.0 copy-done.1
  20.6 0.0 copy-done.6
  20.7 0.7 collective-permute-start.3
  21.4 5.6 %collective-permute-start.2 = (bf16[480,256]{1,0:T(8,128)(2,1)S(1)}, bf16[480,256]{1,0:T(8,128)(2,1)S(1)}, u32[]{:S(2)}, u32[]{:S(2)}) collective-permute-start(bf16[480,256]{1,0:T(8,128)(2,1)S(1)} %get-tuple-element.26), channel_id=1, source_target_pairs={{0,1},{1,0},{2,3},{3,2},{4,5},{5,4},{6,7},{7,6},{8,9},{9,8},{10,11... | collective-permute-start | bytes 737288 | tf_op jit(solution)/shard_map/ppermute | solution.py:369
  27.0 0.0 copy-done.5
  27.0 0.9 %copy.27 = bf16[3,256,256]{2,1,0:T(8,128)(2,1)} copy(bf16[3,256,256]{1,2,0:T(8,128)(2,1)S(1)} %bitcast.70) | data formatting | bytes 786432 | tf_op jit(solution)/shard_map/transpose | solution.py:427
  27.9 0.7 pad_maximum_fusion.3
  28.6 0.7 pad_maximum_fusion
  29.4 0.0 collective-permute-done.3.far
  29.4 0.0 copy-start.9
  29.4 5.9 %collective-permute-done.2.near = bf16[480,256]{1,0:T(8,128)(2,1)S(1)} collective-permute-done((bf16[480,256]{1,0:T(8,128)(2,1)S(1)}, bf16[480,256]{1,0:T(8,128)(2,1)S(1)}, u32[]{:S(2)}, u32[]{:S(2)}) %collective-permute-start.2) | collective-permute-done | bytes 245792 | tf_op jit(solution)/shard_map/ppermute | solution.py:369
  35.3 0.0 copy-start.10
  35.3 0.0 copy-done.9
  35.3 0.7 copy-done.10
  36.0 12.5 %forward.1 = (bf16[2048,256]{1,0:T(8,128)(2,1)}, bf16[256,768]{1,0:T(8,128)(2,1)}, bf16[2304,256]{1,0:T(8,128)(2,1)}, bf16[400,256]{1,0:T(8,128)(2,1)}, bf16[288,256]{1,0:T(8,128)(2,1)}) custom-call(s32[1]{0:T(128)} %bitcast.odd_ref, bf16[480,256]{1,0:T(8,128)(2,1)} %copy-done.10, bf16[480,256]{1,0:T(8,128)(2,1)} %copy-done.9, bf16[2048,256]{1,0:T(8,128)(2,1)} %bitcast.58, ...), custom_call_target="tpu_custom_call" | custom-call | flops 5000000000 | bytes 8000000 | tf_op jit(solution)/shard_map/forward/pallas_call | solution.py:296
  48.5 5.4 %all-to-all-start = ((bf16[32,8,768]{2,1,0:T(8,128)(2,1)}), bf16[32,8,768]{2,1,0:T(8,128)(2,1)S(1)}, u32[]{:S(2)}, u32[]{:S(2)}) async-start(bf16[32,8,768]{2,1,0:T(8,128)(2,1)} %bitcast.72), calls=%async_computation | async-start | bytes 786432 | tf_op jit(solution)/shard_map/all_to_all | solution.py:432
  53.9 0.0 copy-start.3
  53.9 7.2 %backward.1 = bf16[2048,256]{1,0:T(8,128)(2,1)} custom-call(bf16[2304,256]{1,0:T(8,128)(2,1)} %get-tuple-element.12.grad_main_hbm, bf16[400,256]{1,0:T(8,128)(2,1)} %get-tuple-element.13.grad_side_hbm, bf16[288,256]{1,0:T(8,128)(2,1)} %get-tuple-element.14.taps_hbm, bf16[768,256]{1,0:T(8,128)(2,1)} %bitcast.69, bf16[2048,256]{1,0:T(8,128)(2,1)} %bitcast.62), custom_call_target="tpu_custom_call" | custom-call | flops 3000000000 | bytes 5000000 | tf_op jit(solution)/shard_map/backward/pallas_call | solution.py:336
  61.1 8.2 %all-to-all-done = bf16[32,8,768]{2,1,0:T(8,128)(2,1)S(1)} async-done(((bf16[32,8,768]{2,1,0:T(8,128)(2,1)}), bf16[32,8,768]{2,1,0:T(8,128)(2,1)S(1)}, u32[]{:S(2)}, u32[]{:S(2)}) %all-to-all-start) | async-done | bytes 393248 | tf_op jit(solution)/shard_map/all_to_all | solution.py:432
  69.3 0.1 reduce_sum.21
  69.4 0.7 broadcast_in_dim.2
  70.1 0.0 copy-start.4
  70.1 9.3 %all-to-all-start.1 = ((bf16[16,8,768]{2,1,0:T(8,128)(2,1)}), bf16[16,8,768]{2,1,0:T(8,128)(2,1)S(1)}, u32[]{:S(2)}, u32[]{:S(2)}) async-start(bf16[16,8,768]{2,1,0:T(8,128)(2,1)} %broadcast_in_dim.2), calls=%async_computation.1 | async-start | bytes 393216 | tf_op jit(solution)/shard_map/all_to_all | solution.py:442
  79.4 0.0 copy-done.3
  79.4 1.8 %copy.28 = bf16[16,128,256]{1,0,2:T(8,128)(2,1)} copy(bf16[16,128,256]{2,1,0:T(8,128)(2,1)S(1)} %bitcast.63) | data formatting | bytes 2097152 | tf_op jit(solution)/shard_map/reshape | solution.py:445
  81.2 0.0 copy-done.4
  81.2 1.8 %copy.29 = bf16[16,128,256]{1,0,2:T(8,128)(2,1)} copy(bf16[16,128,256]{2,1,0:T(8,128)(2,1)S(1)} %bitcast.64) | data formatting | bytes 2097152 | tf_op jit(solution)/shard_map/reshape | solution.py:446
  83.0 6.9 %all-to-all-done.1 = bf16[16,8,768]{2,1,0:T(8,128)(2,1)S(1)} async-done(((bf16[16,8,768]{2,1,0:T(8,128)(2,1)}), bf16[16,8,768]{2,1,0:T(8,128)(2,1)S(1)}, u32[]{:S(2)}, u32[]{:S(2)}) %all-to-all-start.1) | async-done | bytes 196640 | tf_op jit(solution)/shard_map/all_to_all | solution.py:442
  89.9 0.6 convert_reduce_fusion
  (22 shorter events, 0.3 us)
Async XLA Ops:
  0.6 1.8 %copy-start.2 = (bf16[256,16,128]{2,1,0:T(8,128)(2,1)S(1)}, bf16[256,16,128]{2,1,0:T(8,128)(2,1)}, u32[]{:S(2)}) copy-start(bf16[256,16,128]{2,1,0:T(8,128)(2,1)} %param.7) | copy-start | bytes 3145732
  2.4 17.0 %copy-start = (bf16[256,16,128]{0,2,1:T(8,128)(2,1)}, bf16[256,16,128]{0,2,1:T(8,128)(2,1)S(1)}, u32[]{:S(2)}) copy-start(bf16[256,16,128]{0,2,1:T(8,128)(2,1)S(1)} %copy.23) | copy-start | bytes 3145732
  3.2 17.4 %copy-start.1 = (bf16[256,16,128]{0,2,1:T(8,128)(2,1)}, bf16[256,16,128]{0,2,1:T(8,128)(2,1)S(1)}, u32[]{:S(2)}) copy-start(bf16[256,16,128]{0,2,1:T(8,128)(2,1)S(1)} %copy.24) | copy-start | bytes 3145732
  3.2 16.2 %copy-start.8 = (s32[16,2]{0,1:T(2,128)S(1)}, s32[16,2]{0,1:T(2,128)}, u32[]{:S(2)}) copy-start(s32[16,2]{0,1:T(2,128)} %param.9) | copy-start | bytes 388
  3.3 16.3 %copy-start.7 = (bf16[3,16,3,17]{3,1,2,0:T(8,128)(2,1)S(1)}, bf16[3,16,3,17]{3,1,2,0:T(8,128)(2,1)}, u32[]{:S(2)}) copy-start(bf16[3,16,3,17]{3,1,2,0:T(8,128)(2,1)} %param.8) | copy-start | bytes 14692
  3.4 16.4 %collective-permute-start.1 = (bf16[16,24,256]{2,1,0:T(8,128)(2,1)S(1)}, bf16[16,24,256]{2,1,0:T(8,128)(2,1)S(1)}, u32[]{:S(2)}, u32[]{:S(2)}) collective-permute-start(bf16[16,24,256]{2,1,0:T(8,128)(2,1)S(1)} %get-tuple-element.29), channel_id=1, source_target_pairs={{16,32},{32,16},{48,64},{64,48},{80,96},{96,80},{112,128},{128,112... | collective-permute-start | bytes 589832 | tf_op jit(solution)/shard_map/ppermute | solution.py:370
  7.9 12.5 %collective-permute-start = (bf16[16,24,256]{2,1,0:T(8,128)(2,1)S(1)}, bf16[16,24,256]{2,1,0:T(8,128)(2,1)S(1)}, u32[]{:S(2)}, u32[]{:S(2)}) collective-permute-start(bf16[16,24,256]{2,1,0:T(8,128)(2,1)S(1)} %get-tuple-element.30), channel_id=1, source_target_pairs={{0,16},{16,0},{32,48},{48,32},{64,80},{80,64},{96,112},{112,96},{1... | collective-permute-start | bytes 589832 | tf_op jit(solution)/shard_map/ppermute | solution.py:369
  19.8 0.8 copy-start.6
  20.5 6.5 %copy-start.5 = (bf16[256,3,256]{2,0,1:T(8,128)(2,1)S(1)}, bf16[256,3,256]{2,0,1:T(8,128)(2,1)}, u32[]{:S(2)}) copy-start(bf16[256,3,256]{2,0,1:T(8,128)(2,1)} %param.10) | copy-start | bytes 1179652
  20.7 8.7 %collective-permute-start.3 = (bf16[480,256]{1,0:T(8,128)(2,1)S(1)}, bf16[480,256]{1,0:T(8,128)(2,1)S(1)}, u32[]{:S(2)}, u32[]{:S(2)}) collective-permute-start(bf16[480,256]{1,0:T(8,128)(2,1)S(1)} %get-tuple-element.25), channel_id=1, source_target_pairs={{1,2},{2,1},{3,4},{4,3},{5,6},{6,5},{7,8},{8,7},{9,10},{10,9},{11,... | collective-permute-start | bytes 737288 | tf_op jit(solution)/shard_map/ppermute | solution.py:370
  21.4 13.9 %collective-permute-start.2 = (bf16[480,256]{1,0:T(8,128)(2,1)S(1)}, bf16[480,256]{1,0:T(8,128)(2,1)S(1)}, u32[]{:S(2)}, u32[]{:S(2)}) collective-permute-start(bf16[480,256]{1,0:T(8,128)(2,1)S(1)} %get-tuple-element.26), channel_id=1, source_target_pairs={{0,1},{1,0},{2,3},{3,2},{4,5},{5,4},{6,7},{7,6},{8,9},{9,8},{10,11... | collective-permute-start | bytes 737288 | tf_op jit(solution)/shard_map/ppermute | solution.py:369
  29.4 5.9 %copy-start.9 = (bf16[480,256]{1,0:T(8,128)(2,1)}, bf16[480,256]{1,0:T(8,128)(2,1)S(1)}, u32[]{:S(2)}) copy-start(bf16[480,256]{1,0:T(8,128)(2,1)S(1)} %collective-permute-done.3.far) | copy-start | bytes 737284
  35.3 0.7 copy-start.10
  48.5 20.8 %all-to-all-start = ((bf16[32,8,768]{2,1,0:T(8,128)(2,1)}), bf16[32,8,768]{2,1,0:T(8,128)(2,1)S(1)}, u32[]{:S(2)}, u32[]{:S(2)}) async-start(bf16[32,8,768]{2,1,0:T(8,128)(2,1)} %bitcast.72), calls=%async_computation | async-start | bytes 786432 | tf_op jit(solution)/shard_map/all_to_all | solution.py:432
  53.9 25.5 %copy-start.3 = (bf16[2048,256]{1,0:T(8,128)(2,1)S(1)}, bf16[2048,256]{1,0:T(8,128)(2,1)}, u32[]{:S(2)}) copy-start(bf16[2048,256]{1,0:T(8,128)(2,1)} %get-tuple-element.10) | copy-start | bytes 3145732
  70.1 11.1 %copy-start.4 = (bf16[2048,256]{1,0:T(8,128)(2,1)S(1)}, bf16[2048,256]{1,0:T(8,128)(2,1)}, u32[]{:S(2)}) copy-start(bf16[2048,256]{1,0:T(8,128)(2,1)} %backward.1) | copy-start | bytes 3145732
  70.1 19.8 %all-to-all-start.1 = ((bf16[16,8,768]{2,1,0:T(8,128)(2,1)}), bf16[16,8,768]{2,1,0:T(8,128)(2,1)S(1)}, u32[]{:S(2)}, u32[]{:S(2)}) async-start(bf16[16,8,768]{2,1,0:T(8,128)(2,1)} %broadcast_in_dim.2), calls=%async_computation.1 | async-start | bytes 393216 | tf_op jit(solution)/shard_map/all_to_all | solution.py:442

commit v4 on v3

--- a/solution.py
+++ b/solution.py
@@ -182,7 +182,7 @@
         grad_side[side, :] = (cs[side, :].astype(F32) * slope).astype(BF16)
         return carry
 
-    lax.fori_loop(0, TALL // PACK, step, 0)
+    lax.fori_loop(0, TALL // PACK, step, 0, unroll=True)
     results = [
         pltpu.make_async_copy(src, dst, sem_out.at[i])
         for i, (src, dst) in enumerate(

time: 91 us -> 89.3 us (0.981)
  Pallas kernels: 19.7 us -> 18 us
    pallas_call x1, Pallas kernels: 12.5 us -> 10.8 us  [forward(): pl.pallas_call(forward_kernel, out_shape=(shape(ROWS * COLS, CELL), shape...]
where the time goes in v4:
time: 89.3 us; the launch traced here: 88.8 us
  starting transfers between devices  37 us (41%)
  waiting for transfers between devices  21.7 us (24%)
  Pallas kernels  18 us (20%)
  local copies, waits for them, and re-layouts  8.69 us (10%)
  other arithmetic  2.44 us (3%)
  between operations  1.04 us (1%)
    ppermute x2, starting transfers between devices, swap_pairs(): got_near = lax.ppermute(jnp.where(odd, first, last), axis, near)  17.1 us
    pallas_call x1, Pallas kernels, forward(): pl.pallas_call(forward_kernel, out_shape=(shape(ROWS * COLS, CELL), shape...  10.8 us
    all_to_all x1, starting transfers between devices, body(): lax.all_to_all(jnp.broadcast_to(part[None], (n_lat, share, K * chans)), '...  9.31 us
    all_to_all x1, waiting for transfers between devices, body(): got = lax.all_to_all(term.reshape(n_lon, share, K * chans), 'lon', 0, 0)  8.19 us
    pallas_call x1, Pallas kernels, backward(): pl.pallas_call(backward_kernel, out_shape=shape(ROWS * COLS, CELL), in_sp...  7.2 us
    all_to_all x1, waiting for transfers between devices, body(): lax.all_to_all(jnp.broadcast_to(part[None], (n_lat, share, K * chans)), '...  6.92 us
    ppermute x2, waiting for transfers between devices, swap_pairs(): got_near = lax.ppermute(jnp.where(odd, first, last), axis, near)  6.56 us
    all_to_all x1, starting transfers between devices, body(): got = lax.all_to_all(term.reshape(n_lon, share, K * chans), 'lon', 0, 0)  5.4 us
  transfers between devices with their start and end apart: 6, of which 4 were waited for; matrix products, arithmetic and copies ran while one was open for 7% of the time, Pallas kernels for 8%

profile of v4, /device:TPU:1, one launch (start us, length us, event | category | flops | bytes accessed | tf_op | source)
XLA Modules:
  0.0 88.8 jit_solution(4572880922236940745)
XLA Ops:
  0.6 0.0 copy-start.2
  0.7 1.7 %copy.23 = bf16[256,16,128]{0,2,1:T(8,128)(2,1)S(1)} copy(bf16[256,16,128]{2,1,0:T(8,128)(2,1)} %param.6) | data formatting | bytes 2097152 | tf_op args[0]
  2.4 0.0 copy-start
  2.4 0.0 copy-done.2
  2.4 0.8 copy.24
  3.2 0.0 copy-start.1
  3.2 0.0 copy-start.8
  3.3 0.0 copy-start.7
  3.3 0.1 broadcast_select_fusion.4
  3.4 4.5 %collective-permute-start.1 = (bf16[16,24,256]{2,1,0:T(8,128)(2,1)S(1)}, bf16[16,24,256]{2,1,0:T(8,128)(2,1)S(1)}, u32[]{:S(2)}, u32[]{:S(2)}) collective-permute-start(bf16[16,24,256]{2,1,0:T(8,128)(2,1)S(1)} %get-tuple-element.29), channel_id=1, source_target_pairs={{16,32},{32,16},{48,64},{64,48},{80,96},{96,80},{112,128},{128,112... | collective-permute-start | bytes 589832 | tf_op jit(solution)/shard_map/ppermute | solution.py:370
  7.9 11.5 %collective-permute-start = (bf16[16,24,256]{2,1,0:T(8,128)(2,1)S(1)}, bf16[16,24,256]{2,1,0:T(8,128)(2,1)S(1)}, u32[]{:S(2)}, u32[]{:S(2)}) collective-permute-start(bf16[16,24,256]{2,1,0:T(8,128)(2,1)S(1)} %get-tuple-element.30), channel_id=1, source_target_pairs={{0,16},{16,0},{32,48},{48,32},{64,80},{80,64},{96,112},{112,96},{1... | collective-permute-start | bytes 589832 | tf_op jit(solution)/shard_map/ppermute | solution.py:369
  19.4 0.0 copy-done
  19.5 0.0 copy-done.8
  19.5 0.1 and_convert_fusion
  19.6 0.0 copy-done.7
  19.6 0.1 rev.3
  19.8 0.0 copy-start.6
  19.8 0.0 collective-permute-done.1
  19.8 0.6 collective-permute-done
  20.5 0.0 copy-start.5
  20.6 0.0 copy-done.1
  20.6 0.0 copy-done.6
  20.7 0.7 collective-permute-start.3
  21.4 5.6 %collective-permute-start.2 = (bf16[480,256]{1,0:T(8,128)(2,1)S(1)}, bf16[480,256]{1,0:T(8,128)(2,1)S(1)}, u32[]{:S(2)}, u32[]{:S(2)}) collective-permute-start(bf16[480,256]{1,0:T(8,128)(2,1)S(1)} %get-tuple-element.26), channel_id=1, source_target_pairs={{0,1},{1,0},{2,3},{3,2},{4,5},{5,4},{6,7},{7,6},{8,9},{9,8},{10,11... | collective-permute-start | bytes 737288 | tf_op jit(solution)/shard_map/ppermute | solution.py:369
  27.0 0.0 copy-done.5
  27.0 0.9 %copy.27 = bf16[3,256,256]{2,1,0:T(8,128)(2,1)} copy(bf16[3,256,256]{1,2,0:T(8,128)(2,1)S(1)} %bitcast.70) | data formatting | bytes 786432 | tf_op jit(solution)/shard_map/transpose | solution.py:427
  27.9 0.7 pad_maximum_fusion.3
  28.6 0.7 pad_maximum_fusion
  29.4 0.0 collective-permute-done.3.far
  29.4 0.0 copy-start.9
  29.4 5.9 %collective-permute-done.2.near = bf16[480,256]{1,0:T(8,128)(2,1)S(1)} collective-permute-done((bf16[480,256]{1,0:T(8,128)(2,1)S(1)}, bf16[480,256]{1,0:T(8,128)(2,1)S(1)}, u32[]{:S(2)}, u32[]{:S(2)}) %collective-permute-start.2) | collective-permute-done | bytes 245792 | tf_op jit(solution)/shard_map/ppermute | solution.py:369
  35.3 0.0 copy-start.10
  35.3 0.0 copy-done.9
  35.3 0.7 copy-done.10
  36.0 10.8 %forward.1 = (bf16[2048,256]{1,0:T(8,128)(2,1)}, bf16[256,768]{1,0:T(8,128)(2,1)}, bf16[2304,256]{1,0:T(8,128)(2,1)}, bf16[400,256]{1,0:T(8,128)(2,1)}, bf16[288,256]{1,0:T(8,128)(2,1)}) custom-call(s32[1]{0:T(128)} %bitcast.odd_ref, bf16[480,256]{1,0:T(8,128)(2,1)} %copy-done.10, bf16[480,256]{1,0:T(8,128)(2,1)} %copy-done.9, bf16[2048,256]{1,0:T(8,128)(2,1)} %bitcast.58, ...), custom_call_target="tpu_custom_call" | custom-call | flops 5000000000 | bytes 8000000 | tf_op jit(solution)/shard_map/forward/pallas_call | solution.py:296
  46.8 5.4 %all-to-all-start = ((bf16[32,8,768]{2,1,0:T(8,128)(2,1)}), bf16[32,8,768]{2,1,0:T(8,128)(2,1)S(1)}, u32[]{:S(2)}, u32[]{:S(2)}) async-start(bf16[32,8,768]{2,1,0:T(8,128)(2,1)} %bitcast.72), calls=%async_computation | async-start | bytes 786432 | tf_op jit(solution)/shard_map/all_to_all | solution.py:432
  52.2 0.0 copy-start.3
  52.2 7.2 %backward.1 = bf16[2048,256]{1,0:T(8,128)(2,1)} custom-call(bf16[2304,256]{1,0:T(8,128)(2,1)} %get-tuple-element.12.grad_main_hbm, bf16[400,256]{1,0:T(8,128)(2,1)} %get-tuple-element.13.grad_side_hbm, bf16[288,256]{1,0:T(8,128)(2,1)} %get-tuple-element.14.taps_hbm, bf16[768,256]{1,0:T(8,128)(2,1)} %bitcast.69, bf16[2048,256]{1,0:T(8,128)(2,1)} %bitcast.62), custom_call_target="tpu_custom_call" | custom-call | flops 3000000000 | bytes 5000000 | tf_op jit(solution)/shard_map/backward/pallas_call | solution.py:336
  59.4 8.2 %all-to-all-done = bf16[32,8,768]{2,1,0:T(8,128)(2,1)S(1)} async-done(((bf16[32,8,768]{2,1,0:T(8,128)(2,1)}), bf16[32,8,768]{2,1,0:T(8,128)(2,1)S(1)}, u32[]{:S(2)}, u32[]{:S(2)}) %all-to-all-start) | async-done | bytes 393248 | tf_op jit(solution)/shard_map/all_to_all | solution.py:432
  67.6 0.1 reduce_sum.21
  67.6 0.7 broadcast_in_dim.2
  68.3 0.0 copy-start.4
  68.3 9.3 %all-to-all-start.1 = ((bf16[16,8,768]{2,1,0:T(8,128)(2,1)}), bf16[16,8,768]{2,1,0:T(8,128)(2,1)S(1)}, u32[]{:S(2)}, u32[]{:S(2)}) async-start(bf16[16,8,768]{2,1,0:T(8,128)(2,1)} %broadcast_in_dim.2), calls=%async_computation.1 | async-start | bytes 393216 | tf_op jit(solution)/shard_map/all_to_all | solution.py:442
  77.7 0.0 copy-done.3
  77.7 1.8 %copy.28 = bf16[16,128,256]{1,0,2:T(8,128)(2,1)} copy(bf16[16,128,256]{2,1,0:T(8,128)(2,1)S(1)} %bitcast.63) | data formatting | bytes 2097152 | tf_op jit(solution)/shard_map/reshape | solution.py:445
  79.5 0.0 copy-done.4
  79.5 1.8 %copy.29 = bf16[16,128,256]{1,0,2:T(8,128)(2,1)} copy(bf16[16,128,256]{2,1,0:T(8,128)(2,1)S(1)} %bitcast.64) | data formatting | bytes 2097152 | tf_op jit(solution)/shard_map/reshape | solution.py:446
  81.2 6.9 %all-to-all-done.1 = bf16[16,8,768]{2,1,0:T(8,128)(2,1)S(1)} async-done(((bf16[16,8,768]{2,1,0:T(8,128)(2,1)}), bf16[16,8,768]{2,1,0:T(8,128)(2,1)S(1)}, u32[]{:S(2)}, u32[]{:S(2)}) %all-to-all-start.1) | async-done | bytes 196640 | tf_op jit(solution)/shard_map/all_to_all | solution.py:442
  88.2 0.6 convert_reduce_fusion
  (22 shorter events, 0.3 us)
Async XLA Ops:
  0.6 1.8 %copy-start.2 = (bf16[256,16,128]{2,1,0:T(8,128)(2,1)S(1)}, bf16[256,16,128]{2,1,0:T(8,128)(2,1)}, u32[]{:S(2)}) copy-start(bf16[256,16,128]{2,1,0:T(8,128)(2,1)} %param.7) | copy-start | bytes 3145732
  2.4 17.0 %copy-start = (bf16[256,16,128]{0,2,1:T(8,128)(2,1)}, bf16[256,16,128]{0,2,1:T(8,128)(2,1)S(1)}, u32[]{:S(2)}) copy-start(bf16[256,16,128]{0,2,1:T(8,128)(2,1)S(1)} %copy.23) | copy-start | bytes 3145732
  3.2 17.4 %copy-start.1 = (bf16[256,16,128]{0,2,1:T(8,128)(2,1)}, bf16[256,16,128]{0,2,1:T(8,128)(2,1)S(1)}, u32[]{:S(2)}) copy-start(bf16[256,16,128]{0,2,1:T(8,128)(2,1)S(1)} %copy.24) | copy-start | bytes 3145732
  3.2 16.2 %copy-start.8 = (s32[16,2]{0,1:T(2,128)S(1)}, s32[16,2]{0,1:T(2,128)}, u32[]{:S(2)}) copy-start(s32[16,2]{0,1:T(2,128)} %param.9) | copy-start | bytes 388
  3.3 16.3 %copy-start.7 = (bf16[3,16,3,17]{3,1,2,0:T(8,128)(2,1)S(1)}, bf16[3,16,3,17]{3,1,2,0:T(8,128)(2,1)}, u32[]{:S(2)}) copy-start(bf16[3,16,3,17]{3,1,2,0:T(8,128)(2,1)} %param.8) | copy-start | bytes 14692
  3.4 16.4 %collective-permute-start.1 = (bf16[16,24,256]{2,1,0:T(8,128)(2,1)S(1)}, bf16[16,24,256]{2,1,0:T(8,128)(2,1)S(1)}, u32[]{:S(2)}, u32[]{:S(2)}) collective-permute-start(bf16[16,24,256]{2,1,0:T(8,128)(2,1)S(1)} %get-tuple-element.29), channel_id=1, source_target_pairs={{16,32},{32,16},{48,64},{64,48},{80,96},{96,80},{112,128},{128,112... | collective-permute-start | bytes 589832 | tf_op jit(solution)/shard_map/ppermute | solution.py:370
  7.9 12.5 %collective-permute-start = (bf16[16,24,256]{2,1,0:T(8,128)(2,1)S(1)}, bf16[16,24,256]{2,1,0:T(8,128)(2,1)S(1)}, u32[]{:S(2)}, u32[]{:S(2)}) collective-permute-start(bf16[16,24,256]{2,1,0:T(8,128)(2,1)S(1)} %get-tuple-element.30), channel_id=1, source_target_pairs={{0,16},{16,0},{32,48},{48,32},{64,80},{80,64},{96,112},{112,96},{1... | collective-permute-start | bytes 589832 | tf_op jit(solution)/shard_map/ppermute | solution.py:369
  19.8 0.8 copy-start.6
  20.5 6.5 %copy-start.5 = (bf16[256,3,256]{2,0,1:T(8,128)(2,1)S(1)}, bf16[256,3,256]{2,0,1:T(8,128)(2,1)}, u32[]{:S(2)}) copy-start(bf16[256,3,256]{2,0,1:T(8,128)(2,1)} %param.10) | copy-start | bytes 1179652
  20.7 8.7 %collective-permute-start.3 = (bf16[480,256]{1,0:T(8,128)(2,1)S(1)}, bf16[480,256]{1,0:T(8,128)(2,1)S(1)}, u32[]{:S(2)}, u32[]{:S(2)}) collective-permute-start(bf16[480,256]{1,0:T(8,128)(2,1)S(1)} %get-tuple-element.25), channel_id=1, source_target_pairs={{1,2},{2,1},{3,4},{4,3},{5,6},{6,5},{7,8},{8,7},{9,10},{10,9},{11,... | collective-permute-start | bytes 737288 | tf_op jit(solution)/shard_map/ppermute | solution.py:370
  21.4 13.9 %collective-permute-start.2 = (bf16[480,256]{1,0:T(8,128)(2,1)S(1)}, bf16[480,256]{1,0:T(8,128)(2,1)S(1)}, u32[]{:S(2)}, u32[]{:S(2)}) collective-permute-start(bf16[480,256]{1,0:T(8,128)(2,1)S(1)} %get-tuple-element.26), channel_id=1, source_target_pairs={{0,1},{1,0},{2,3},{3,2},{4,5},{5,4},{6,7},{7,6},{8,9},{9,8},{10,11... | collective-permute-start | bytes 737288 | tf_op jit(solution)/shard_map/ppermute | solution.py:369
  29.4 5.9 %copy-start.9 = (bf16[480,256]{1,0:T(8,128)(2,1)}, bf16[480,256]{1,0:T(8,128)(2,1)S(1)}, u32[]{:S(2)}) copy-start(bf16[480,256]{1,0:T(8,128)(2,1)S(1)} %collective-permute-done.3.far) | copy-start | bytes 737284
  35.3 0.7 copy-start.10
  46.8 20.8 %all-to-all-start = ((bf16[32,8,768]{2,1,0:T(8,128)(2,1)}), bf16[32,8,768]{2,1,0:T(8,128)(2,1)S(1)}, u32[]{:S(2)}, u32[]{:S(2)}) async-start(bf16[32,8,768]{2,1,0:T(8,128)(2,1)} %bitcast.72), calls=%async_computation | async-start | bytes 786432 | tf_op jit(solution)/shard_map/all_to_all | solution.py:432
  52.2 25.5 %copy-start.3 = (bf16[2048,256]{1,0:T(8,128)(2,1)S(1)}, bf16[2048,256]{1,0:T(8,128)(2,1)}, u32[]{:S(2)}) copy-start(bf16[2048,256]{1,0:T(8,128)(2,1)} %get-tuple-element.10) | copy-start | bytes 3145732
  68.3 11.1 %copy-start.4 = (bf16[2048,256]{1,0:T(8,128)(2,1)S(1)}, bf16[2048,256]{1,0:T(8,128)(2,1)}, u32[]{:S(2)}) copy-start(bf16[2048,256]{1,0:T(8,128)(2,1)} %backward.1) | copy-start | bytes 3145732
  68.3 19.8 %all-to-all-start.1 = ((bf16[16,8,768]{2,1,0:T(8,128)(2,1)}), bf16[16,8,768]{2,1,0:T(8,128)(2,1)S(1)}, u32[]{:S(2)}, u32[]{:S(2)}) async-start(bf16[16,8,768]{2,1,0:T(8,128)(2,1)} %broadcast_in_dim.2), calls=%async_computation.1 | async-start | bytes 393216 | tf_op jit(solution)/shard_map/all_to_all | solution.py:442

commit v5 on v4

--- a/solution.py
+++ b/solution.py
@@ -182,20 +182,29 @@
         grad_side[side, :] = (cs[side, :].astype(F32) * slope).astype(BF16)
         return carry
 
-    lax.fori_loop(0, TALL // PACK, step, 0, unroll=True)
+    size = PACK * COLS
+    pieces = []
+    for group in range(TALL // PACK):
+        low_line = max(group * size, COLS)
+        high_line = min((group + 1) * size, (TALL - 1) * COLS)
+        pieces.append(
+            (
+                out.at[pl.ds(low_line, high_line - low_line)],
+                out_hbm.at[pl.ds(low_line - COLS, high_line - low_line)],
+            )
+        )
+        pieces.append(
+            (grad_main.at[pl.ds(group * size, size)], grad_main_hbm.at[pl.ds(group * size, size)])
+        )
+    pieces += [(grad_side, grad_side_hbm), (taps_all, taps_hbm), (term, term_hbm)]
     results = [
-        pltpu.make_async_copy(src, dst, sem_out.at[i])
-        for i, (src, dst) in enumerate(
-            (
-                (out.at[pl.ds(COLS, ROWS * COLS)], out_hbm),
-                (grad_main, grad_main_hbm),
-                (grad_side, grad_side_hbm),
-                (taps_all, taps_hbm),
-                (term, term_hbm),
-            )
-        )
+        pltpu.make_async_copy(src, dst, sem_out.at[i]) for i, (src, dst) in enumerate(pieces)
     ]
-    for copy in results[:4]:
+    for group in range(TALL // PACK):
+        step(group, 0)
+        for copy in results[2 * group : 2 * group + 2]:
+            copy.start()
+    for copy in results[-3:-1]:
         copy.start()
     total = lax.dot_general(
         grad_main[COLS : COLS + ROWS * COLS, :],
@@ -204,7 +213,7 @@
         preferred_element_type=F32,
     )
     term[...] = (total * scale_ref[0]).astype(BF16)
-    results[4].start()
+    results[-1].start()
     for copy in results:
         copy.wait()
 
@@ -322,7 +331,7 @@
             pltpu.SemaphoreType.DMA((6,)),
             pltpu.SemaphoreType.DMA((5,)),
             pltpu.SemaphoreType.DMA((5,)),
-            pltpu.SemaphoreType.DMA((5,)),
+            pltpu.SemaphoreType.DMA((9,)),
         ],
         compiler_params=pltpu.CompilerParams(vmem_limit_bytes=60 * 2**20),
         cost_estimate=pl.CostEstimate(

time: 89.3 us -> 89.3 us (level)
  no operation moved by 1% of the time
where the time goes in v5:
time: 89.3 us; the launch traced here: 88.8 us
  starting transfers between devices  37 us (41%)
  waiting for transfers between devices  21.7 us (24%)
  Pallas kernels  18 us (20%)
  local copies, waits for them, and re-layouts  8.69 us (10%)
  other arithmetic  2.44 us (3%)
  between operations  1.04 us (1%)
    ppermute x2, starting transfers between devices, swap_pairs(): got_near = lax.ppermute(jnp.where(odd, first, last), axis, near)  17.1 us
    pallas_call x1, Pallas kernels, forward(): pl.pallas_call(forward_kernel, out_shape=(shape(ROWS * COLS, CELL), shape...  10.8 us
    all_to_all x1, starting transfers between devices, body(): lax.all_to_all(jnp.broadcast_to(part[None], (n_lat, share, K * chans)), '...  9.32 us
    all_to_all x1, waiting for transfers between devices, body(): got = lax.all_to_all(term.reshape(n_lon, share, K * chans), 'lon', 0, 0)  8.19 us
    pallas_call x1, Pallas kernels, backward(): pl.pallas_call(backward_kernel, out_shape=shape(ROWS * COLS, CELL), in_sp...  7.2 us
    all_to_all x1, waiting for transfers between devices, body(): lax.all_to_all(jnp.broadcast_to(part[None], (n_lat, share, K * chans)), '...  6.92 us
    ppermute x2, waiting for transfers between devices, swap_pairs(): got_near = lax.ppermute(jnp.where(odd, first, last), axis, near)  6.56 us
    all_to_all x1, starting transfers between devices, body(): got = lax.all_to_all(term.reshape(n_lon, share, K * chans), 'lon', 0, 0)  5.4 us
  transfers between devices with their start and end apart: 6, of which 4 were waited for; matrix products, arithmetic and copies ran while one was open for 7% of the time, Pallas kernels for 8%

profile of v5, /device:TPU:1, one launch (start us, length us, event | category | flops | bytes accessed | tf_op | source)
XLA Modules:
  0.0 88.8 jit_solution(14881088571781168191)
XLA Ops:
  0.6 0.0 copy-start.2
  0.7 1.7 %copy.23 = bf16[256,16,128]{0,2,1:T(8,128)(2,1)S(1)} copy(bf16[256,16,128]{2,1,0:T(8,128)(2,1)} %param.6) | data formatting | bytes 2097152 | tf_op args[0]
  2.4 0.0 copy-start
  2.4 0.0 copy-done.2
  2.4 0.8 copy.24
  3.2 0.0 copy-start.1
  3.2 0.0 copy-start.8
  3.3 0.0 copy-start.7
  3.3 0.1 broadcast_select_fusion.4
  3.4 4.5 %collective-permute-start.1 = (bf16[16,24,256]{2,1,0:T(8,128)(2,1)S(1)}, bf16[16,24,256]{2,1,0:T(8,128)(2,1)S(1)}, u32[]{:S(2)}, u32[]{:S(2)}) collective-permute-start(bf16[16,24,256]{2,1,0:T(8,128)(2,1)S(1)} %get-tuple-element.29), channel_id=1, source_target_pairs={{16,32},{32,16},{48,64},{64,48},{80,96},{96,80},{112,128},{128,112... | collective-permute-start | bytes 589832 | tf_op jit(solution)/shard_map/ppermute | solution.py:379
  7.9 11.5 %collective-permute-start = (bf16[16,24,256]{2,1,0:T(8,128)(2,1)S(1)}, bf16[16,24,256]{2,1,0:T(8,128)(2,1)S(1)}, u32[]{:S(2)}, u32[]{:S(2)}) collective-permute-start(bf16[16,24,256]{2,1,0:T(8,128)(2,1)S(1)} %get-tuple-element.30), channel_id=1, source_target_pairs={{0,16},{16,0},{32,48},{48,32},{64,80},{80,64},{96,112},{112,96},{1... | collective-permute-start | bytes 589832 | tf_op jit(solution)/shard_map/ppermute | solution.py:378
  19.4 0.0 copy-done
  19.5 0.0 copy-done.8
  19.5 0.1 and_convert_fusion
  19.6 0.0 copy-done.7
  19.6 0.1 rev.3
  19.8 0.0 copy-start.6
  19.8 0.0 collective-permute-done.1
  19.8 0.6 collective-permute-done
  20.5 0.0 copy-start.5
  20.6 0.0 copy-done.1
  20.6 0.0 copy-done.6
  20.7 0.7 collective-permute-start.3
  21.4 5.6 %collective-permute-start.2 = (bf16[480,256]{1,0:T(8,128)(2,1)S(1)}, bf16[480,256]{1,0:T(8,128)(2,1)S(1)}, u32[]{:S(2)}, u32[]{:S(2)}) collective-permute-start(bf16[480,256]{1,0:T(8,128)(2,1)S(1)} %get-tuple-element.26), channel_id=1, source_target_pairs={{0,1},{1,0},{2,3},{3,2},{4,5},{5,4},{6,7},{7,6},{8,9},{9,8},{10,11... | collective-permute-start | bytes 737288 | tf_op jit(solution)/shard_map/ppermute | solution.py:378
  27.0 0.0 copy-done.5
  27.0 0.9 %copy.27 = bf16[3,256,256]{2,1,0:T(8,128)(2,1)} copy(bf16[3,256,256]{1,2,0:T(8,128)(2,1)S(1)} %bitcast.70) | data formatting | bytes 786432 | tf_op jit(solution)/shard_map/transpose | solution.py:436
  27.9 0.7 pad_maximum_fusion.3
  28.6 0.7 pad_maximum_fusion
  29.4 0.0 collective-permute-done.3.far
  29.4 0.0 copy-start.9
  29.4 5.9 %collective-permute-done.2.near = bf16[480,256]{1,0:T(8,128)(2,1)S(1)} collective-permute-done((bf16[480,256]{1,0:T(8,128)(2,1)S(1)}, bf16[480,256]{1,0:T(8,128)(2,1)S(1)}, u32[]{:S(2)}, u32[]{:S(2)}) %collective-permute-start.2) | collective-permute-done | bytes 245792 | tf_op jit(solution)/shard_map/ppermute | solution.py:378
  35.3 0.0 copy-start.10
  35.3 0.0 copy-done.9
  35.3 0.7 copy-done.10
  36.0 10.8 %forward.1 = (bf16[2048,256]{1,0:T(8,128)(2,1)}, bf16[256,768]{1,0:T(8,128)(2,1)}, bf16[2304,256]{1,0:T(8,128)(2,1)}, bf16[400,256]{1,0:T(8,128)(2,1)}, bf16[288,256]{1,0:T(8,128)(2,1)}) custom-call(s32[1]{0:T(128)} %bitcast.odd_ref, bf16[480,256]{1,0:T(8,128)(2,1)} %copy-done.10, bf16[480,256]{1,0:T(8,128)(2,1)} %copy-done.9, bf16[2048,256]{1,0:T(8,128)(2,1)} %bitcast.58, ...), custom_call_target="tpu_custom_call" | custom-call | flops 5000000000 | bytes 8000000 | tf_op jit(solution)/shard_map/forward/pallas_call | solution.py:305
  46.8 5.4 %all-to-all-start = ((bf16[32,8,768]{2,1,0:T(8,128)(2,1)}), bf16[32,8,768]{2,1,0:T(8,128)(2,1)S(1)}, u32[]{:S(2)}, u32[]{:S(2)}) async-start(bf16[32,8,768]{2,1,0:T(8,128)(2,1)} %bitcast.72), calls=%async_computation | async-start | bytes 786432 | tf_op jit(solution)/shard_map/all_to_all | solution.py:441
  52.2 0.0 copy-start.3
  52.2 7.2 %backward.1 = bf16[2048,256]{1,0:T(8,128)(2,1)} custom-call(bf16[2304,256]{1,0:T(8,128)(2,1)} %get-tuple-element.12.grad_main_hbm, bf16[400,256]{1,0:T(8,128)(2,1)} %get-tuple-element.13.grad_side_hbm, bf16[288,256]{1,0:T(8,128)(2,1)} %get-tuple-element.14.taps_hbm, bf16[768,256]{1,0:T(8,128)(2,1)} %bitcast.69, bf16[2048,256]{1,0:T(8,128)(2,1)} %bitcast.62), custom_call_target="tpu_custom_call" | custom-call | flops 3000000000 | bytes 5000000 | tf_op jit(solution)/shard_map/backward/pallas_call | solution.py:345
  59.4 8.2 %all-to-all-done = bf16[32,8,768]{2,1,0:T(8,128)(2,1)S(1)} async-done(((bf16[32,8,768]{2,1,0:T(8,128)(2,1)}), bf16[32,8,768]{2,1,0:T(8,128)(2,1)S(1)}, u32[]{:S(2)}, u32[]{:S(2)}) %all-to-all-start) | async-done | bytes 393248 | tf_op jit(solution)/shard_map/all_to_all | solution.py:441
  67.6 0.1 reduce_sum.21
  67.6 0.7 broadcast_in_dim.2
  68.3 0.0 copy-start.4
  68.3 9.3 %all-to-all-start.1 = ((bf16[16,8,768]{2,1,0:T(8,128)(2,1)}), bf16[16,8,768]{2,1,0:T(8,128)(2,1)S(1)}, u32[]{:S(2)}, u32[]{:S(2)}) async-start(bf16[16,8,768]{2,1,0:T(8,128)(2,1)} %broadcast_in_dim.2), calls=%async_computation.1 | async-start | bytes 393216 | tf_op jit(solution)/shard_map/all_to_all | solution.py:451
  77.7 0.0 copy-done.3
  77.7 1.8 %copy.28 = bf16[16,128,256]{1,0,2:T(8,128)(2,1)} copy(bf16[16,128,256]{2,1,0:T(8,128)(2,1)S(1)} %bitcast.63) | data formatting | bytes 2097152 | tf_op jit(solution)/shard_map/reshape | solution.py:454
  79.5 0.0 copy-done.4
  79.5 1.8 %copy.29 = bf16[16,128,256]{1,0,2:T(8,128)(2,1)} copy(bf16[16,128,256]{2,1,0:T(8,128)(2,1)S(1)} %bitcast.64) | data formatting | bytes 2097152 | tf_op jit(solution)/shard_map/reshape | solution.py:455
  81.2 6.9 %all-to-all-done.1 = bf16[16,8,768]{2,1,0:T(8,128)(2,1)S(1)} async-done(((bf16[16,8,768]{2,1,0:T(8,128)(2,1)}), bf16[16,8,768]{2,1,0:T(8,128)(2,1)S(1)}, u32[]{:S(2)}, u32[]{:S(2)}) %all-to-all-start.1) | async-done | bytes 196640 | tf_op jit(solution)/shard_map/all_to_all | solution.py:451
  88.2 0.6 convert_reduce_fusion
  (22 shorter events, 0.3 us)
Async XLA Ops:
  0.6 1.8 %copy-start.2 = (bf16[256,16,128]{2,1,0:T(8,128)(2,1)S(1)}, bf16[256,16,128]{2,1,0:T(8,128)(2,1)}, u32[]{:S(2)}) copy-start(bf16[256,16,128]{2,1,0:T(8,128)(2,1)} %param.7) | copy-start | bytes 3145732
  2.4 17.0 %copy-start = (bf16[256,16,128]{0,2,1:T(8,128)(2,1)}, bf16[256,16,128]{0,2,1:T(8,128)(2,1)S(1)}, u32[]{:S(2)}) copy-start(bf16[256,16,128]{0,2,1:T(8,128)(2,1)S(1)} %copy.23) | copy-start | bytes 3145732
  3.2 17.4 %copy-start.1 = (bf16[256,16,128]{0,2,1:T(8,128)(2,1)}, bf16[256,16,128]{0,2,1:T(8,128)(2,1)S(1)}, u32[]{:S(2)}) copy-start(bf16[256,16,128]{0,2,1:T(8,128)(2,1)S(1)} %copy.24) | copy-start | bytes 3145732
  3.2 16.2 %copy-start.8 = (s32[16,2]{0,1:T(2,128)S(1)}, s32[16,2]{0,1:T(2,128)}, u32[]{:S(2)}) copy-start(s32[16,2]{0,1:T(2,128)} %param.9) | copy-start | bytes 388
  3.3 16.3 %copy-start.7 = (bf16[3,16,3,17]{3,1,2,0:T(8,128)(2,1)S(1)}, bf16[3,16,3,17]{3,1,2,0:T(8,128)(2,1)}, u32[]{:S(2)}) copy-start(bf16[3,16,3,17]{3,1,2,0:T(8,128)(2,1)} %param.8) | copy-start | bytes 14692
  3.4 16.4 %collective-permute-start.1 = (bf16[16,24,256]{2,1,0:T(8,128)(2,1)S(1)}, bf16[16,24,256]{2,1,0:T(8,128)(2,1)S(1)}, u32[]{:S(2)}, u32[]{:S(2)}) collective-permute-start(bf16[16,24,256]{2,1,0:T(8,128)(2,1)S(1)} %get-tuple-element.29), channel_id=1, source_target_pairs={{16,32},{32,16},{48,64},{64,48},{80,96},{96,80},{112,128},{128,112... | collective-permute-start | bytes 589832 | tf_op jit(solution)/shard_map/ppermute | solution.py:379
  7.9 12.5 %collective-permute-start = (bf16[16,24,256]{2,1,0:T(8,128)(2,1)S(1)}, bf16[16,24,256]{2,1,0:T(8,128)(2,1)S(1)}, u32[]{:S(2)}, u32[]{:S(2)}) collective-permute-start(bf16[16,24,256]{2,1,0:T(8,128)(2,1)S(1)} %get-tuple-element.30), channel_id=1, source_target_pairs={{0,16},{16,0},{32,48},{48,32},{64,80},{80,64},{96,112},{112,96},{1... | collective-permute-start | bytes 589832 | tf_op jit(solution)/shard_map/ppermute | solution.py:378
  19.8 0.8 copy-start.6
  20.5 6.5 %copy-start.5 = (bf16[256,3,256]{2,0,1:T(8,128)(2,1)S(1)}, bf16[256,3,256]{2,0,1:T(8,128)(2,1)}, u32[]{:S(2)}) copy-start(bf16[256,3,256]{2,0,1:T(8,128)(2,1)} %param.10) | copy-start | bytes 1179652
  20.7 8.7 %collective-permute-start.3 = (bf16[480,256]{1,0:T(8,128)(2,1)S(1)}, bf16[480,256]{1,0:T(8,128)(2,1)S(1)}, u32[]{:S(2)}, u32[]{:S(2)}) collective-permute-start(bf16[480,256]{1,0:T(8,128)(2,1)S(1)} %get-tuple-element.25), channel_id=1, source_target_pairs={{1,2},{2,1},{3,4},{4,3},{5,6},{6,5},{7,8},{8,7},{9,10},{10,9},{11,... | collective-permute-start | bytes 737288 | tf_op jit(solution)/shard_map/ppermute | solution.py:379
  21.4 13.9 %collective-permute-start.2 = (bf16[480,256]{1,0:T(8,128)(2,1)S(1)}, bf16[480,256]{1,0:T(8,128)(2,1)S(1)}, u32[]{:S(2)}, u32[]{:S(2)}) collective-permute-start(bf16[480,256]{1,0:T(8,128)(2,1)S(1)} %get-tuple-element.26), channel_id=1, source_target_pairs={{0,1},{1,0},{2,3},{3,2},{4,5},{5,4},{6,7},{7,6},{8,9},{9,8},{10,11... | collective-permute-start | bytes 737288 | tf_op jit(solution)/shard_map/ppermute | solution.py:378
  29.4 5.9 %copy-start.9 = (bf16[480,256]{1,0:T(8,128)(2,1)}, bf16[480,256]{1,0:T(8,128)(2,1)S(1)}, u32[]{:S(2)}) copy-start(bf16[480,256]{1,0:T(8,128)(2,1)S(1)} %collective-permute-done.3.far) | copy-start | bytes 737284
  35.3 0.7 copy-start.10
  46.8 20.8 %all-to-all-start = ((bf16[32,8,768]{2,1,0:T(8,128)(2,1)}), bf16[32,8,768]{2,1,0:T(8,128)(2,1)S(1)}, u32[]{:S(2)}, u32[]{:S(2)}) async-start(bf16[32,8,768]{2,1,0:T(8,128)(2,1)} %bitcast.72), calls=%async_computation | async-start | bytes 786432 | tf_op jit(solution)/shard_map/all_to_all | solution.py:441
  52.2 25.5 %copy-start.3 = (bf16[2048,256]{1,0:T(8,128)(2,1)S(1)}, bf16[2048,256]{1,0:T(8,128)(2,1)}, u32[]{:S(2)}) copy-start(bf16[2048,256]{1,0:T(8,128)(2,1)} %get-tuple-element.10) | copy-start | bytes 3145732
  68.3 11.1 %copy-start.4 = (bf16[2048,256]{1,0:T(8,128)(2,1)S(1)}, bf16[2048,256]{1,0:T(8,128)(2,1)}, u32[]{:S(2)}) copy-start(bf16[2048,256]{1,0:T(8,128)(2,1)} %backward.1) | copy-start | bytes 3145732
  68.3 19.8 %all-to-all-start.1 = ((bf16[16,8,768]{2,1,0:T(8,128)(2,1)}), bf16[16,8,768]{2,1,0:T(8,128)(2,1)S(1)}, u32[]{:S(2)}, u32[]{:S(2)}) async-start(bf16[16,8,768]{2,1,0:T(8,128)(2,1)} %broadcast_in_dim.2), calls=%async_computation.1 | async-start | bytes 393216 | tf_op jit(solution)/shard_map/all_to_all | solution.py:451
